TPU v7x, 32 devices: a whole 2x2x4 slice. The times are simulated.
32 devices in a mesh: seq: 4 (over z), head: 4 (over x, core), batch: 2 (over y).
Axes of the slice: x: 2, y: 2, z: 4, core: 2. Of those that a mesh axis runs over, the one named last changes fastest.
Arguments:
- tokens: bfloat16 [8, 1024, 1024], P('batch', 'seq'), may hold values from -6 to 6
- cotangent: bfloat16 [8, 1024, 1024], P('batch', 'seq'), may hold values from -6 to 6
- prefix: float32 [2, 64, 1024], P(None, None, 'head'), may hold values from -6 to 6
- first_moment: float32 [2, 64, 1024], P(None, None, 'head'), may hold values from -6 to 6
- second_moment: float32 [2, 64, 1024], P(None, None, 'head'), may hold values from 6.784 to 26.88
- w_qkv: bfloat16 [3, 1024, 1024], P(None, None, 'head'), may hold values from -0.1875 to 0.1875
- proj_bias: float32 [3, 1024], P(None, 'head'), may hold values from -4 to 4
- w_out: bfloat16 [1024, 1024], P('head'), may hold values from -1.5 to 1.5
- w_in: bfloat16 [1024, 4096], P(None, 'head'), may hold values from -0.1875 to 0.1875
- ffn_bias: float32 [4096], P('head'), may hold values from -4 to 4
- w_down: bfloat16 [4096, 1024], P('head'), may hold values from -0.09375 to 0.09375
- gains: float32 [2, 1024], replicated, may hold values from 0.5 to 1.5
- shifts: float32 [4, 1024], replicated, may hold values from -4 to 4
- lengths: int32 [8], P('batch'), may hold values from 32 to 1024, as said below
- key_mask: int32 [8, 1024], P('batch', 'seq'), may hold values 0 or 1
Outputs:
- layer_out: float32 [8, 1024, 1024], P('batch', 'seq')
- input_grad: float32 [8, 1024, 1024], P('batch', 'seq')
- prefix_grad: float32 [2, 64, 1024], P(None, None, 'head')
- new_prefix: float32 [2, 64, 1024], P(None, None, 'head')
- new_first: float32 [2, 64, 1024], P(None, None, 'head')
- new_second: float32 [2, 64, 1024], P(None, None, 'head')
Inputs may be any that keep to these rules, and one draw needn't show every extreme that they name: `lengths`: one sequence of every draw has the length 1024.
All inputs are finite; a program needn't handle non-finite values. No bound on the sum of `key_mask` on one device may be relied on, other than what follows from the above.
Results may differ from a plain program's by a relative error of at most 0.029.
Values may be sent and summed in bfloat16 or wider, within the bound.
A program may use at most 128 MiB of HBM per device.

v0:
```python
import jax
import jax.numpy as jnp
from jax import lax
from jax.sharding import PartitionSpec as P

HEAD_DIM = 64
STEP = 10


NEG_FILL = -1e30
NORM_EPSILON = 1e-05
BETA_ONE = 0.9
BETA_TWO = 0.95
LEARN_RATE = 0.8
WEIGHT_DECAY = 0.01
ADAM_EPSILON = 1e-08


def shifted(value, axis, steps):
    count = lax.axis_size(axis)
    pairs = [(source, (source + steps) % count) for source in range(count)]
    return lax.ppermute(value, axis, pairs)


def layer_norm(values_in, gain_row, shift_row):
    row_mean = jnp.mean(values_in, axis=-1, keepdims=True)
    centred = values_in - row_mean
    spread = jnp.mean(centred * centred, axis=-1, keepdims=True)
    return centred * lax.rsqrt(spread + NORM_EPSILON) * gain_row + shift_row


def exact_gelu(values_in):
    return jax.nn.gelu(values_in, approximate=False)


def block_scores(queries, block_keys, block_bias, score_scale):
    scores = (
        jnp.einsum("shqd,shkd->shqk", queries, block_keys, preferred_element_type=jnp.float32)
        * score_scale
    )
    return scores + block_bias.astype(jnp.float32)[:, None, None, :]


def absorb(softmax_state, queries, block_keys, block_values, block_bias, score_scale):
    row_max, row_sum, weighted = softmax_state
    scores = block_scores(queries, block_keys, block_bias, score_scale)
    new_max = jnp.maximum(row_max, jnp.max(scores, axis=-1))
    fade_factor = jnp.exp(row_max - new_max)
    exp_scores = jnp.exp(scores - new_max[..., None])
    row_sum = row_sum * fade_factor + jnp.sum(exp_scores, axis=-1)
    weighted = weighted * fade_factor[..., None] + jnp.einsum(
        "shqk,shkd->shqd",
        exp_scores.astype(jnp.bfloat16),
        block_values,
        preferred_element_type=jnp.float32,
    )
    return (new_max, row_sum, weighted)


def back_block(
    queries, grad_att, log_total, row_delta, block_keys, block_values, block_bias, score_scale
):
    scores = block_scores(queries, block_keys, block_bias, score_scale)
    probabilities = jnp.exp(scores - log_total[..., None])
    grad_probs = jnp.einsum(
        "shqd,shkd->shqk", grad_att, block_values, preferred_element_type=jnp.float32
    )
    grad_scores = (probabilities * (grad_probs - row_delta[..., None])).astype(jnp.bfloat16)
    grad_queries = (
        jnp.einsum("shqk,shkd->shqd", grad_scores, block_keys, preferred_element_type=jnp.float32)
        * score_scale
    )
    grad_keys = (
        jnp.einsum("shqk,shqd->shkd", grad_scores, queries, preferred_element_type=jnp.float32)
        * score_scale
    )
    grad_values = jnp.einsum(
        "shqk,shqd->shkd",
        probabilities.astype(jnp.bfloat16),
        grad_att,
        preferred_element_type=jnp.float32,
    )
    return (grad_queries, grad_keys, grad_values)


def body(
    tokens,
    cotangent,
    prefix,
    first_moment,
    second_moment,
    w_qkv,
    proj_bias,
    w_out,
    w_in,
    ffn_bias,
    w_down,
    gains,
    shifts,
    lengths,
    key_mask,
):
    seqs_dev, shard_len, model_width = tokens.shape
    row_count = seqs_dev * shard_len
    local_width = w_qkv.shape[2]
    heads_dev = local_width // HEAD_DIM
    prefix_slots = prefix.shape[1]
    score_scale = HEAD_DIM ** (-0.5)
    cycle_size = lax.axis_size("seq")
    cycle_place = lax.axis_index("seq")
    flat_tokens = tokens.reshape(row_count, model_width)
    projected = (
        jnp.einsum("td,ide->ite", flat_tokens, w_qkv, preferred_element_type=jnp.float32)
        + proj_bias[:, None, :]
    )
    by_head = (
        projected.astype(jnp.bfloat16)
        .reshape(3, seqs_dev, shard_len, heads_dev, HEAD_DIM)
        .transpose(0, 1, 3, 2, 4)
    )
    queries = by_head[0]
    own_keys = by_head[1]
    own_values = by_head[2]
    positions = cycle_place * shard_len + lax.broadcasted_iota(jnp.int32, (seqs_dev, shard_len), 1)
    live_keys = (key_mask == 1) & (positions < lengths[:, None])
    own_bias = jnp.where(live_keys, 0.0, NEG_FILL).astype(jnp.bfloat16)
    prefix_low = (
        prefix.astype(jnp.bfloat16)
        .reshape(2, prefix_slots, heads_dev, HEAD_DIM)
        .transpose(0, 2, 1, 3)
    )
    pre_scores = (
        jnp.einsum("shqd,hpd->shqp", queries, prefix_low[0], preferred_element_type=jnp.float32)
        * score_scale
    )
    row_max = jnp.max(pre_scores, axis=-1)
    exp_prefix = jnp.exp(pre_scores - row_max[..., None])
    row_sum = jnp.sum(exp_prefix, axis=-1)
    weighted = jnp.einsum(
        "shqp,hpd->shqd",
        exp_prefix.astype(jnp.bfloat16),
        prefix_low[1],
        preferred_element_type=jnp.float32,
    )

    def visit_keys(softmax_state, block_keys, block_values, block_bias):
        return absorb(softmax_state, queries, block_keys, block_values, block_bias, score_scale)

    def forward_turn(turn_index, carried):
        softmax_state, block_keys, block_values, block_bias = carried
        softmax_state = visit_keys(softmax_state, block_keys, block_values, block_bias)
        block_keys, block_values, block_bias = shifted(
            (block_keys, block_values, block_bias), "seq", 1
        )
        return (softmax_state, block_keys, block_values, block_bias)

    carried = lax.fori_loop(
        0,
        cycle_size - 1,
        forward_turn,
        ((row_max, row_sum, weighted), own_keys, own_values, own_bias),
    )
    row_max, row_sum, weighted = visit_keys(carried[0], carried[1], carried[2], carried[3])
    log_total = row_max + jnp.log(row_sum)
    attended = weighted / row_sum[..., None]
    merged = attended.astype(jnp.bfloat16).transpose(0, 2, 1, 3).reshape(row_count, local_width)
    attention = (
        lax.psum(jnp.dot(merged, w_out, preferred_element_type=jnp.float32), "head") + shifts[0]
    )
    resid_one = flat_tokens.astype(jnp.float32) + attention
    normed, norm_one_back = jax.vjp(
        lambda values_in: layer_norm(values_in, gains[0], shifts[1]), resid_one
    )
    inner_sum = (
        jnp.dot(normed.astype(jnp.bfloat16), w_in, preferred_element_type=jnp.float32) + ffn_bias
    )
    activated, gelu_back = jax.vjp(exact_gelu, inner_sum)
    feed_forward = (
        lax.psum(
            jnp.dot(activated.astype(jnp.bfloat16), w_down, preferred_element_type=jnp.float32),
            "head",
        )
        + shifts[2]
    )
    layer_value, norm_two_back = jax.vjp(
        lambda values_in: layer_norm(values_in, gains[1], shifts[3]), normed + feed_forward
    )
    contract_last = (((1,), (1,)), ((), ()))
    (grad_two,) = norm_two_back(cotangent.reshape(row_count, model_width).astype(jnp.float32))
    grad_act = lax.dot_general(
        grad_two.astype(jnp.bfloat16), w_down, contract_last, preferred_element_type=jnp.float32
    )
    (grad_inner,) = gelu_back(grad_act)
    hidden_part = lax.dot_general(
        grad_inner.astype(jnp.bfloat16), w_in, contract_last, preferred_element_type=jnp.float32
    )
    grad_normed = grad_two + lax.psum(hidden_part, "head")
    (grad_one,) = norm_one_back(grad_normed)
    grad_merged = lax.dot_general(
        grad_one.astype(jnp.bfloat16), w_out, contract_last, preferred_element_type=jnp.float32
    )
    grad_att = (
        grad_merged.astype(jnp.bfloat16)
        .reshape(seqs_dev, shard_len, heads_dev, HEAD_DIM)
        .transpose(0, 2, 1, 3)
    )
    row_delta = jnp.sum(grad_att.astype(jnp.float32) * attended, axis=-1)
    pre_probs = jnp.exp(pre_scores - log_total[..., None])
    grad_pre_probs = jnp.einsum(
        "shqd,hpd->shqp", grad_att, prefix_low[1], preferred_element_type=jnp.float32
    )
    grad_pre_scores = (pre_probs * (grad_pre_probs - row_delta[..., None])).astype(jnp.bfloat16)
    grad_query_pre = (
        jnp.einsum(
            "shqp,hpd->shqd", grad_pre_scores, prefix_low[0], preferred_element_type=jnp.float32
        )
        * score_scale
    )
    grad_pre_keys = (
        jnp.einsum("shqp,shqd->hpd", grad_pre_scores, queries, preferred_element_type=jnp.float32)
        * score_scale
    )
    grad_pre_values = jnp.einsum(
        "shqp,shqd->hpd",
        pre_probs.astype(jnp.bfloat16),
        grad_att,
        preferred_element_type=jnp.float32,
    )
    prefix_terms = (
        jnp.stack([grad_pre_keys, grad_pre_values])
        .transpose(0, 2, 1, 3)
        .reshape(2, prefix_slots, local_width)
    )
    empty_grad = jnp.zeros(queries.shape, jnp.float32)

    def back_visit(query_side, key_side):
        return back_block(
            query_side[0],
            query_side[1],
            query_side[2],
            query_side[3],
            key_side[0],
            key_side[1],
            key_side[2],
            score_scale,
        )

    own_key_side = (own_keys, own_values, own_bias)

    def query_turn(turn_index, carried):
        grad_keys, grad_values, visit_queries, visit_grad, visit_total, visit_delta, visit_sum = (
            carried
        )
        turn_queries, turn_keys, turn_values = back_visit(
            (visit_queries, visit_grad, visit_total, visit_delta), own_key_side
        )
        moved = (
            shifted(visit_queries.astype(jnp.float32), "seq", 1).astype(visit_queries.dtype),
            shifted(visit_grad.astype(jnp.float32), "seq", 1).astype(visit_grad.dtype),
            shifted(visit_total, "seq", 1),
            shifted(visit_delta, "seq", 1),
            shifted(visit_sum + turn_queries, "seq", 1),
        )
        return (grad_keys + turn_keys, grad_values + turn_values) + moved

    carried = lax.fori_loop(
        0,
        cycle_size - 1,
        query_turn,
        (empty_grad, empty_grad, queries, grad_att, log_total, row_delta, grad_query_pre),
    )
    grad_keys, grad_values, visit_queries, visit_grad, visit_total, visit_delta, visit_sum = carried
    turn_queries, turn_keys, turn_values = back_visit(
        (visit_queries, visit_grad, visit_total, visit_delta), own_key_side
    )
    grad_keys = grad_keys + turn_keys
    grad_values = grad_values + turn_values
    grad_queries = shifted(visit_sum + turn_queries, "seq", 1)
    grad_rows = (
        jnp.stack([grad_queries, grad_keys, grad_values])
        .astype(jnp.bfloat16)
        .transpose(0, 1, 3, 2, 4)
        .reshape(3, row_count, local_width)
    )
    input_part = jnp.einsum("ite,ide->td", grad_rows, w_qkv, preferred_element_type=jnp.float32)
    input_grad = grad_one + lax.psum(input_part, "head")
    prefix_grad = lax.psum(prefix_terms, ("seq", "batch"))
    new_first = BETA_ONE * first_moment + (1.0 - BETA_ONE) * prefix_grad
    new_second = BETA_TWO * second_moment + (1.0 - BETA_TWO) * prefix_grad * prefix_grad
    first_hat = new_first / (1.0 - BETA_ONE**STEP)
    second_hat = new_second / (1.0 - BETA_TWO**STEP)
    new_prefix = prefix - LEARN_RATE * (
        first_hat / (jnp.sqrt(second_hat) + ADAM_EPSILON) + WEIGHT_DECAY * prefix
    )
    layer_out = layer_value.reshape(seqs_dev, shard_len, model_width)
    return (
        layer_out,
        input_grad.reshape(seqs_dev, shard_len, model_width),
        prefix_grad,
        new_prefix,
        new_first,
        new_second,
    )


def solution(mesh):
    placed = (
        P("batch", "seq", None),
        P("batch", "seq", None),
        P(None, None, "head"),
        P(None, None, "head"),
        P(None, None, "head"),
        P(None, None, "head"),
        P(None, "head"),
        P("head", None),
        P(None, "head"),
        P("head"),
        P("head", None),
        P(),
        P(),
        P("batch"),
        P("batch", "seq"),
    )
    return jax.shard_map(
        body,
        mesh=mesh,
        in_specs=placed,
        out_specs=(
            P("batch", "seq", None),
            P("batch", "seq", None),
            P(None, None, "head"),
            P(None, None, "head"),
            P(None, None, "head"),
            P(None, None, "head"),
        ),
        check_vma=False,
    )
```

profile of v0, /device:TPU:0, one launch (start us, length us, event | category | flops | bytes accessed | tf_op | source)
XLA Modules:
  0.0 751.7 jit_solution(5014034474601775552)
XLA Ops:
  8.4 5.1 fusion.61
  13.5 3.9 reshape.112
  26.5 83.2 %while.43 = (s32[]{:T(128)}, f32[4,4,256]{2,1,0:T(4,128)S(1)}, f32[4,4,256]{2,1,0:T(4,128)S(1)}, f32[4,4,256,64]{2,3,1,0:T(8,128)}, bf16[4,4,256,64]{2,3,1,0:T(8...) while((s32[]{:T(128)}, f32[4,4,256]{2,1,0:T(4,128)S(1)}, ...), condition=%wide.region_5.6_spmd, body=%wide.region_2.5_spmd.sunk | while | flops 280503296 | bytes 31226124 | solution.py:157
  27.5 3.0 collective-permute-start
  37.6 2.3 fusion.185
  40.9 14.9 %collective-permute-done.2 = bf16[4,256]{1,0:T(4,128)(2,1)S(1)} collective-permute-done((bf16[4,256]{1,0:T(4,128)(2,1)S(1)}, bf16[4,256]{1,0:T(4,128)(2,1)S(1)}, u32[]{:S(2)}, u32[]{:S(2)}) %collective-permute-start.2) | collective-permute-done | bytes 2080 | tf_op jit(solution)/shard_map/while/body/eval_jaxpr/ppermute | solution.py:22
  63.7 2.3 fusion.185
  67.0 16.2 %collective-permute-done.2 = bf16[4,256]{1,0:T(4,128)(2,1)S(1)} collective-permute-done((bf16[4,256]{1,0:T(4,128)(2,1)S(1)}, bf16[4,256]{1,0:T(4,128)(2,1)S(1)}, u32[]{:S(2)}, u32[]{:S(2)}) %collective-permute-start.2) | collective-permute-done | bytes 2080 | tf_op jit(solution)/shard_map/while/body/eval_jaxpr/ppermute | solution.py:22
  88.9 2.3 fusion.185
  92.2 17.4 %collective-permute-done.2 = bf16[4,256]{1,0:T(4,128)(2,1)S(1)} collective-permute-done((bf16[4,256]{1,0:T(4,128)(2,1)S(1)}, bf16[4,256]{1,0:T(4,128)(2,1)S(1)}, u32[]{:S(2)}, u32[]{:S(2)}) %collective-permute-start.2) | collective-permute-done | bytes 2080 | tf_op jit(solution)/shard_map/while/body/eval_jaxpr/ppermute | solution.py:22
  109.7 2.2 fusion.33
  112.9 2.2 fusion.87
  116.7 2.8 fusion.124
  120.3 82.6 %all-reduce.6.cloned.1.call-done = f32[1024,1024]{1,0:T(8,128)} async-done(((f32[1024,1024]{1,0:T(8,128)}), f32[1024,1024]{1,0:T(8,128)}) %all-reduce.6.cloned.1.call-update) | async-done | bytes 4194320 | tf_op jit(solution)/shard_map/psum | solution.py:168
  202.9 3.5 fusion.119
  207.1 10.6 %fusion.24 = (f32[1024,1024]{1,0:T(8,128)S(1)}, f32[1024,1024]{1,0:T(8,128)S(1)}) fusion(f32[1024]{0:T(1024)S(1)} %copy-done.35, bf16[1024,1024]{1,0:T(8,128)(2,1)S(1)} %copy-done, f32[1024,1024]{1,0:T(8,128)S(1)} %get-tuple-element.279, f32[1024]{0:T(1024)S(1)} %bitcast.232, f32[1024]{0:T(1024)S(1)} %bitcast.225, f32[1024]{0:T(1024)S(1)} %fusion.100, ...), kind=kOutput, calls=%fused_computation.29 | convolution fusion | flops 2218786816 | bytes 14700544 | tf_op jit(solution)/shard_map/dot_general | solution.py:175
  221.0 4.6 fusion.46
  225.6 85.7 %all-reduce.8.cloned.1.call-done = f32[1024,1024]{1,0:T(8,128)} async-done(((f32[1024,1024]{1,0:T(8,128)}), f32[1024,1024]{1,0:T(8,128)}) %all-reduce.8.cloned.1.call-update) | async-done | bytes 4194320 | tf_op jit(solution)/shard_map/psum | solution.py:179
  311.4 4.4 fusion.118
  317.0 4.5 fusion.117
  321.5 12.1 %fusion.80 = f32[1024,1024]{1,0:T(8,128)} fusion(bf16[1024,1024]{1,0:T(8,128)(2,1)S(1)} %copy-done, f32[1024,1024]{1,0:T(8,128)} %copy-done.36, f32[1024,1024]{1,0:T(8,128)} %copy-done.37, bf16[1024,1024]{1,0:T(8,128)(2,1)} %param.29, f32[1024,1024]{1,0:T(8,128)} %get-tuple-element.275, f32[1024]{0:T(1024)S(1)} %negate_multiply_fusion.2, ...), kind=kOutput, calls=%fused_computation.112 | convolution fusion | flops 4312793088 | bytes 20979712 | tf_op jit(solution)/shard_map/dot_general | solution.py:194
  333.9 85.5 %all-reduce.10.cloned.1.call-done = f32[1024,1024]{1,0:T(8,128)} async-done(((f32[1024,1024]{1,0:T(8,128)}), f32[1024,1024]{1,0:T(8,128)}) %all-reduce.10.cloned.1.call-update) | async-done | bytes 4194320 | tf_op jit(solution)/shard_map/psum | solution.py:197
  419.4 5.5 multiply_reduce_fusion
  433.2 2.1 reshape.129
  443.3 179.9 %while.44 = (s32[]{:T(128)}, f32[4,4,256,64]{2,3,1,0:T(8,128)}, f32[4,4,256,64]{2,3,1,0:T(8,128)}, bf16[4,4,256,64]{2,3,1,0:T(8,128)(2,1)S(1)}, bf16[4,4,256,64]...) while((s32[]{:T(128)}, f32[4,4,256,64]{2,3,1,0:T(8,128)}, ...), condition=%wide.region_21.22_spmd.clone, body=%wide.region_20.21_spmd.clone.sunk | while | flops 683410432 | bytes 58456452 | solution.py:266
  447.1 3.0 multiply_convert_fusion.5
  450.0 3.1 fusion.199
  459.6 4.4 fusion.198
  465.4 38.3 %collective-permute-done.5 = f32[4,4,256]{2,1,0:T(4,128)S(1)} collective-permute-done((f32[4,4,256]{2,1,0:T(4,128)S(1)}, f32[4,4,256]{2,1,0:T(4,128)S(1)}, u32[]{:S(2)}, u32[]{:S(2)}) %collective-permute-start.5) | collective-permute-done | bytes 16416 | tf_op jit(solution)/shard_map/while/body/eval_jaxpr/ppermute | solution.py:22
  507.8 3.0 multiply_convert_fusion.5
  510.7 3.1 fusion.199
  516.5 2.3 collective-permute-start.5
  518.8 4.6 fusion.198
  523.5 2.7 fusion.197
  526.2 38.3 %collective-permute-done.5 = f32[4,4,256]{2,1,0:T(4,128)S(1)} collective-permute-done((f32[4,4,256]{2,1,0:T(4,128)S(1)}, f32[4,4,256]{2,1,0:T(4,128)S(1)}, u32[]{:S(2)}, u32[]{:S(2)}) %collective-permute-start.5) | collective-permute-done | bytes 16416 | tf_op jit(solution)/shard_map/while/body/eval_jaxpr/ppermute | solution.py:22
  568.6 2.9 multiply_convert_fusion.5
  571.5 3.1 fusion.199
  575.6 4.0 collective-permute-start.5
  579.7 4.6 fusion.198
  584.3 2.7 fusion.197
  587.0 35.9 %collective-permute-done.5 = f32[4,4,256]{2,1,0:T(4,128)S(1)} collective-permute-done((f32[4,4,256]{2,1,0:T(4,128)S(1)}, f32[4,4,256]{2,1,0:T(4,128)S(1)}, u32[]{:S(2)}, u32[]{:S(2)}) %collective-permute-start.5) | collective-permute-done | bytes 16416 | tf_op jit(solution)/shard_map/while/body/eval_jaxpr/ppermute | solution.py:22
  625.0 2.6 multiply_convert_fusion.1
  633.9 8.9 %collective-permute-done.8 = bf16[4,4,256,64]{2,3,1,0:T(8,128)(2,1)S(1)} collective-permute-done((bf16[4,4,256,64]{2,3,1,0:T(8,128)(2,1)S(1)}, bf16[4,4,256,64]{2,3,1,0:T(8,128)(2,1)S(1)}, u32[]{:S(2)}, u32[]{:S(2)}) %collective-permute-start.8) | collective-permute-done | bytes 524320 | tf_op jit(solution)/shard_map/ppermute | solution.py:22
  643.0 2.4 copy.116
  645.3 2.8 reshape.131
  648.2 5.3 convolution_bitcast_fusion
  656.3 81.7 %all-reduce.12.cloned.1.call-done = f32[1024,1024]{1,0:T(8,128)} async-done(((f32[1024,1024]{1,0:T(8,128)}), f32[1024,1024]{1,0:T(8,128)}) %all-reduce.12.cloned.1.call-update) | async-done | bytes 4194320 | tf_op jit(solution)/shard_map/psum | solution.py:286
  738.1 6.0 add_add_fusion.4
  (250 shorter events, 94.9 us)
Async XLA Ops:
  7.2 199.8 %copy-start = (bf16[1024,1024]{1,0:T(8,128)(2,1)S(1)}, bf16[1024,1024]{1,0:T(8,128)(2,1)}, u32[]{:S(2)}) copy-start(bf16[1024,1024]{1,0:T(8,128)(2,1)} %param.27) | copy-start | bytes 6291460
  7.2 195.7 %all-reduce.6.cloned.1.call-start = ((), (), s32[]{:S(2)}) async-start(), calls=%async_computation | async-start | bytes 8388608 | tf_op jit(solution)/shard_map/psum | solution.py:168
  20.9 4.7 copy-start.16
  20.9 4.7 copy-start.18
  20.9 4.7 copy-start.22
  20.9 4.9 copy-start.32
  20.9 4.9 copy-start.33
  27.5 28.3 %collective-permute-start = (bf16[4,4,256,64]{2,3,1,0:T(8,128)(2,1)S(1)}, bf16[4,4,256,64]{2,3,1,0:T(8,128)(2,1)}, u32[]{:S(2)}, u32[]{:S(2)}) collective-permute-start(bf16[4,4,256,64]{2,3,1,0:T(8,128)(2,1)S(1)} %copy.170), channel_id=1, source_target_pairs={{0,8},{8,16},{16,24},{24,0},{1,9},{9,17},{17,25},{25,1},{2,10},{10... | collective-permute-start | bytes 1572872 | tf_op jit(solution)/shard_map/while/body/eval_jaxpr/ppermute | solution.py:22
  32.4 23.4 %collective-permute-start.1 = (bf16[4,4,256,64]{2,3,1,0:T(8,128)(2,1)}, bf16[4,4,256,64]{2,3,1,0:T(8,128)(2,1)}, u32[]{:S(2)}, u32[]{:S(2)}) collective-permute-start(bf16[4,4,256,64]{2,3,1,0:T(8,128)(2,1)} %copy.171), channel_id=1, source_target_pairs={{0,8},{8,16},{16,24},{24,0},{1,9},{9,17},{17,25},{25,1},{2,10},{10... | collective-permute-start | bytes 1572872 | tf_op jit(solution)/shard_map/while/body/eval_jaxpr/ppermute | solution.py:22
  34.0 21.8 %collective-permute-start.2 = (bf16[4,256]{1,0:T(4,128)(2,1)S(1)}, bf16[4,256]{1,0:T(4,128)(2,1)S(1)}, u32[]{:S(2)}, u32[]{:S(2)}) collective-permute-start(bf16[4,256]{1,0:T(4,128)(2,1)S(1)} %copy.172), channel_id=1, source_target_pairs={{0,8},{8,16},{16,24},{24,0},{1,9},{9,17},{17,25},{25,1},{2,10},{10... | collective-permute-start | bytes 6152 | tf_op jit(solution)/shard_map/while/body/eval_jaxpr/ppermute | solution.py:22
  56.9 26.3 %collective-permute-start = (bf16[4,4,256,64]{2,3,1,0:T(8,128)(2,1)S(1)}, bf16[4,4,256,64]{2,3,1,0:T(8,128)(2,1)}, u32[]{:S(2)}, u32[]{:S(2)}) collective-permute-start(bf16[4,4,256,64]{2,3,1,0:T(8,128)(2,1)S(1)} %copy.170), channel_id=1, source_target_pairs={{0,8},{8,16},{16,24},{24,0},{1,9},{9,17},{17,25},{25,1},{2,10},{10... | collective-permute-start | bytes 1572872 | tf_op jit(solution)/shard_map/while/body/eval_jaxpr/ppermute | solution.py:22
  58.8 24.4 %collective-permute-start.1 = (bf16[4,4,256,64]{2,3,1,0:T(8,128)(2,1)}, bf16[4,4,256,64]{2,3,1,0:T(8,128)(2,1)}, u32[]{:S(2)}, u32[]{:S(2)}) collective-permute-start(bf16[4,4,256,64]{2,3,1,0:T(8,128)(2,1)} %copy.171), channel_id=1, source_target_pairs={{0,8},{8,16},{16,24},{24,0},{1,9},{9,17},{17,25},{25,1},{2,10},{10... | collective-permute-start | bytes 1572872 | tf_op jit(solution)/shard_map/while/body/eval_jaxpr/ppermute | solution.py:22
  60.1 23.1 %collective-permute-start.2 = (bf16[4,256]{1,0:T(4,128)(2,1)S(1)}, bf16[4,256]{1,0:T(4,128)(2,1)S(1)}, u32[]{:S(2)}, u32[]{:S(2)}) collective-permute-start(bf16[4,256]{1,0:T(4,128)(2,1)S(1)} %copy.172), channel_id=1, source_target_pairs={{0,8},{8,16},{16,24},{24,0},{1,9},{9,17},{17,25},{25,1},{2,10},{10... | collective-permute-start | bytes 6152 | tf_op jit(solution)/shard_map/while/body/eval_jaxpr/ppermute | solution.py:22
  84.2 25.4 %collective-permute-start = (bf16[4,4,256,64]{2,3,1,0:T(8,128)(2,1)S(1)}, bf16[4,4,256,64]{2,3,1,0:T(8,128)(2,1)}, u32[]{:S(2)}, u32[]{:S(2)}) collective-permute-start(bf16[4,4,256,64]{2,3,1,0:T(8,128)(2,1)S(1)} %copy.170), channel_id=1, source_target_pairs={{0,8},{8,16},{16,24},{24,0},{1,9},{9,17},{17,25},{25,1},{2,10},{10... | collective-permute-start | bytes 1572872 | tf_op jit(solution)/shard_map/while/body/eval_jaxpr/ppermute | solution.py:22
  86.1 23.5 %collective-permute-start.1 = (bf16[4,4,256,64]{2,3,1,0:T(8,128)(2,1)}, bf16[4,4,256,64]{2,3,1,0:T(8,128)(2,1)}, u32[]{:S(2)}, u32[]{:S(2)}) collective-permute-start(bf16[4,4,256,64]{2,3,1,0:T(8,128)(2,1)} %copy.171), channel_id=1, source_target_pairs={{0,8},{8,16},{16,24},{24,0},{1,9},{9,17},{17,25},{25,1},{2,10},{10... | collective-permute-start | bytes 1572872 | tf_op jit(solution)/shard_map/while/body/eval_jaxpr/ppermute | solution.py:22
  86.2 23.5 %collective-permute-start.2 = (bf16[4,256]{1,0:T(4,128)(2,1)S(1)}, bf16[4,256]{1,0:T(4,128)(2,1)S(1)}, u32[]{:S(2)}, u32[]{:S(2)}) collective-permute-start(bf16[4,256]{1,0:T(4,128)(2,1)S(1)} %copy.172), channel_id=1, source_target_pairs={{0,8},{8,16},{16,24},{24,0},{1,9},{9,17},{17,25},{25,1},{2,10},{10... | collective-permute-start | bytes 6152 | tf_op jit(solution)/shard_map/while/body/eval_jaxpr/ppermute | solution.py:22
  119.5 191.8 %all-reduce.8.cloned.1.call-start = ((), (), s32[]{:S(2)}) async-start(), calls=%async_computation.1 | async-start | bytes 8388608 | tf_op jit(solution)/shard_map/psum | solution.py:179
  206.4 11.3 %copy-start.3 = (f32[1024,1024]{1,0:T(8,128)}, f32[1024,1024]{1,0:T(8,128)S(1)}, u32[]{:S(2)}) copy-start(f32[1024,1024]{1,0:T(8,128)S(1)} %get-tuple-element.279) | copy-start | bytes 12582916
  207.1 13.9 %copy-start.34 = (bf16[1024,1024]{1,0:T(8,128)(2,1)S(1)}, bf16[1024,1024]{1,0:T(8,128)(2,1)}, u32[]{:S(2)}) copy-start(bf16[1024,1024]{1,0:T(8,128)(2,1)} %param.29) | copy-start | bytes 6291460
  225.6 193.7 %all-reduce.10.cloned.1.call-start = ((), (), s32[]{:S(2)}) async-start(), calls=%async_computation.2 | async-start | bytes 8388608 | tf_op jit(solution)/shard_map/psum | solution.py:197
  311.4 4.4 copy-start.15
  333.6 319.9 %all-reduce.14.cloned.1.call-start = ((), (), s32[]{:S(2)}) async-start(), calls=%async_computation.4 | async-start | bytes 262144 | tf_op jit(solution)/shard_map/psum | solution.py:287
  419.3 5.8 copy-start.4
  419.3 7.1 copy-start.6
  419.4 8.3 %copy-start.13 = (f32[1024,1024]{1,0:T(8,128)S(1)}, f32[1024,1024]{1,0:T(8,128)}, u32[]{:S(2)}) copy-start(f32[1024,1024]{1,0:T(8,128)} %all-reduce.10.cloned.1.call-done) | copy-start | bytes 12582916
  433.2 5.5 copy-start.11
  442.1 296.0 %all-reduce.12.cloned.1.call-start = ((), (), s32[]{:S(2)}) async-start(), calls=%async_computation.3 | async-start | bytes 8388608 | tf_op jit(solution)/shard_map/psum | solution.py:286
  447.1 6.1 copy-start.2
  453.2 50.7 %collective-permute-start.7 = (f32[4,4,256,64]{2,3,1,0:T(8,128)}, f32[4,4,256,64]{2,3,1,0:T(8,128)}, u32[]{:S(2)}, u32[]{:S(2)}) collective-permute-start(f32[4,4,256,64]{2,3,1,0:T(8,128)} %fusion.199), channel_id=1, source_target_pairs={{0,8},{8,16},{16,24},{24,0},{1,9},{9,17},{17,25},{25,1},{2,10},{10... | collective-permute-start | bytes 3145736 | tf_op jit(solution)/shard_map/while/body/eval_jaxpr/ppermute | solution.py:22
  454.6 49.3 %collective-permute-start.3 = (bf16[4,4,256,64]{2,3,1,0:T(8,128)(2,1)S(1)}, bf16[4,4,256,64]{2,3,1,0:T(8,128)(2,1)S(1)}, u32[]{:S(2)}, u32[]{:S(2)}) collective-permute-start(bf16[4,4,256,64]{2,3,1,0:T(8,128)(2,1)S(1)} %copy.194), channel_id=1, source_target_pairs={{0,8},{8,16},{16,24},{24,0},{1,9},{9,17},{17,25},{25,1},{2,10},{10... | collective-permute-start | bytes 1572872 | tf_op jit(solution)/shard_map/while/body/eval_jaxpr/ppermute | solution.py:22
  456.1 47.8 %collective-permute-start.4 = (bf16[4,4,256,64]{2,3,1,0:T(8,128)(2,1)}, bf16[4,4,256,64]{2,3,1,0:T(8,128)(2,1)}, u32[]{:S(2)}, u32[]{:S(2)}) collective-permute-start(bf16[4,4,256,64]{2,3,1,0:T(8,128)(2,1)} %copy.195), channel_id=1, source_target_pairs={{0,8},{8,16},{16,24},{24,0},{1,9},{9,17},{17,25},{25,1},{2,10},{10... | collective-permute-start | bytes 1572872 | tf_op jit(solution)/shard_map/while/body/eval_jaxpr/ppermute | solution.py:22
  457.6 46.1 %collective-permute-start.5 = (f32[4,4,256]{2,1,0:T(4,128)S(1)}, f32[4,4,256]{2,1,0:T(4,128)S(1)}, u32[]{:S(2)}, u32[]{:S(2)}) collective-permute-start(f32[4,4,256]{2,1,0:T(4,128)S(1)} %copy.196), channel_id=1, source_target_pairs={{0,8},{8,16},{16,24},{24,0},{1,9},{9,17},{17,25},{25,1},{2,10},{10... | collective-permute-start | bytes 49160 | tf_op jit(solution)/shard_map/while/body/eval_jaxpr/ppermute | solution.py:22
  458.1 45.8 %collective-permute-start.6 = (f32[4,4,256]{2,1,0:T(4,128)S(1)}, f32[4,4,256]{2,1,0:T(4,128)S(1)}, u32[]{:S(2)}, u32[]{:S(2)}) collective-permute-start(f32[4,4,256]{2,1,0:T(4,128)S(1)} %copy.197), channel_id=1, source_target_pairs={{0,8},{8,16},{16,24},{24,0},{1,9},{9,17},{17,25},{25,1},{2,10},{10... | collective-permute-start | bytes 49160 | tf_op jit(solution)/shard_map/while/body/eval_jaxpr/ppermute | solution.py:22
  507.7 6.1 copy-start.2
  513.8 50.9 %collective-permute-start.7 = (f32[4,4,256,64]{2,3,1,0:T(8,128)}, f32[4,4,256,64]{2,3,1,0:T(8,128)}, u32[]{:S(2)}, u32[]{:S(2)}) collective-permute-start(f32[4,4,256,64]{2,3,1,0:T(8,128)} %fusion.199), channel_id=1, source_target_pairs={{0,8},{8,16},{16,24},{24,0},{1,9},{9,17},{17,25},{25,1},{2,10},{10... | collective-permute-start | bytes 3145736 | tf_op jit(solution)/shard_map/while/body/eval_jaxpr/ppermute | solution.py:22
  513.8 50.9 %collective-permute-start.3 = (bf16[4,4,256,64]{2,3,1,0:T(8,128)(2,1)S(1)}, bf16[4,4,256,64]{2,3,1,0:T(8,128)(2,1)S(1)}, u32[]{:S(2)}, u32[]{:S(2)}) collective-permute-start(bf16[4,4,256,64]{2,3,1,0:T(8,128)(2,1)S(1)} %copy.194), channel_id=1, source_target_pairs={{0,8},{8,16},{16,24},{24,0},{1,9},{9,17},{17,25},{25,1},{2,10},{10... | collective-permute-start | bytes 1572872 | tf_op jit(solution)/shard_map/while/body/eval_jaxpr/ppermute | solution.py:22
  515.0 49.7 %collective-permute-start.4 = (bf16[4,4,256,64]{2,3,1,0:T(8,128)(2,1)}, bf16[4,4,256,64]{2,3,1,0:T(8,128)(2,1)}, u32[]{:S(2)}, u32[]{:S(2)}) collective-permute-start(bf16[4,4,256,64]{2,3,1,0:T(8,128)(2,1)} %copy.195), channel_id=1, source_target_pairs={{0,8},{8,16},{16,24},{24,0},{1,9},{9,17},{17,25},{25,1},{2,10},{10... | collective-permute-start | bytes 1572872 | tf_op jit(solution)/shard_map/while/body/eval_jaxpr/ppermute | solution.py:22
  516.5 48.0 %collective-permute-start.5 = (f32[4,4,256]{2,1,0:T(4,128)S(1)}, f32[4,4,256]{2,1,0:T(4,128)S(1)}, u32[]{:S(2)}, u32[]{:S(2)}) collective-permute-start(f32[4,4,256]{2,1,0:T(4,128)S(1)} %copy.196), channel_id=1, source_target_pairs={{0,8},{8,16},{16,24},{24,0},{1,9},{9,17},{17,25},{25,1},{2,10},{10... | collective-permute-start | bytes 49160 | tf_op jit(solution)/shard_map/while/body/eval_jaxpr/ppermute | solution.py:22
  518.8 45.9 %collective-permute-start.6 = (f32[4,4,256]{2,1,0:T(4,128)S(1)}, f32[4,4,256]{2,1,0:T(4,128)S(1)}, u32[]{:S(2)}, u32[]{:S(2)}) collective-permute-start(f32[4,4,256]{2,1,0:T(4,128)S(1)} %copy.197), channel_id=1, source_target_pairs={{0,8},{8,16},{16,24},{24,0},{1,9},{9,17},{17,25},{25,1},{2,10},{10... | collective-permute-start | bytes 49160 | tf_op jit(solution)/shard_map/while/body/eval_jaxpr/ppermute | solution.py:22
  568.6 6.1 copy-start.2
  574.7 48.5 %collective-permute-start.7 = (f32[4,4,256,64]{2,3,1,0:T(8,128)}, f32[4,4,256,64]{2,3,1,0:T(8,128)}, u32[]{:S(2)}, u32[]{:S(2)}) collective-permute-start(f32[4,4,256,64]{2,3,1,0:T(8,128)} %fusion.199), channel_id=1, source_target_pairs={{0,8},{8,16},{16,24},{24,0},{1,9},{9,17},{17,25},{25,1},{2,10},{10... | collective-permute-start | bytes 3145736 | tf_op jit(solution)/shard_map/while/body/eval_jaxpr/ppermute | solution.py:22
  574.7 48.5 %collective-permute-start.3 = (bf16[4,4,256,64]{2,3,1,0:T(8,128)(2,1)S(1)}, bf16[4,4,256,64]{2,3,1,0:T(8,128)(2,1)S(1)}, u32[]{:S(2)}, u32[]{:S(2)}) collective-permute-start(bf16[4,4,256,64]{2,3,1,0:T(8,128)(2,1)S(1)} %copy.194), channel_id=1, source_target_pairs={{0,8},{8,16},{16,24},{24,0},{1,9},{9,17},{17,25},{25,1},{2,10},{10... | collective-permute-start | bytes 1572872 | tf_op jit(solution)/shard_map/while/body/eval_jaxpr/ppermute | solution.py:22
  574.7 48.5 %collective-permute-start.4 = (bf16[4,4,256,64]{2,3,1,0:T(8,128)(2,1)}, bf16[4,4,256,64]{2,3,1,0:T(8,128)(2,1)}, u32[]{:S(2)}, u32[]{:S(2)}) collective-permute-start(bf16[4,4,256,64]{2,3,1,0:T(8,128)(2,1)} %copy.195), channel_id=1, source_target_pairs={{0,8},{8,16},{16,24},{24,0},{1,9},{9,17},{17,25},{25,1},{2,10},{10... | collective-permute-start | bytes 1572872 | tf_op jit(solution)/shard_map/while/body/eval_jaxpr/ppermute | solution.py:22
  575.6 47.3 %collective-permute-start.5 = (f32[4,4,256]{2,1,0:T(4,128)S(1)}, f32[4,4,256]{2,1,0:T(4,128)S(1)}, u32[]{:S(2)}, u32[]{:S(2)}) collective-permute-start(f32[4,4,256]{2,1,0:T(4,128)S(1)} %copy.196), channel_id=1, source_target_pairs={{0,8},{8,16},{16,24},{24,0},{1,9},{9,17},{17,25},{25,1},{2,10},{10... | collective-permute-start | bytes 49160 | tf_op jit(solution)/shard_map/while/body/eval_jaxpr/ppermute | solution.py:22
  579.6 43.5 %collective-permute-start.6 = (f32[4,4,256]{2,1,0:T(4,128)S(1)}, f32[4,4,256]{2,1,0:T(4,128)S(1)}, u32[]{:S(2)}, u32[]{:S(2)}) collective-permute-start(f32[4,4,256]{2,1,0:T(4,128)S(1)} %copy.197), channel_id=1, source_target_pairs={{0,8},{8,16},{16,24},{24,0},{1,9},{9,17},{17,25},{25,1},{2,10},{10... | collective-permute-start | bytes 49160 | tf_op jit(solution)/shard_map/while/body/eval_jaxpr/ppermute | solution.py:22
  629.4 13.4 %collective-permute-start.8 = (bf16[4,4,256,64]{2,3,1,0:T(8,128)(2,1)S(1)}, bf16[4,4,256,64]{2,3,1,0:T(8,128)(2,1)S(1)}, u32[]{:S(2)}, u32[]{:S(2)}) collective-permute-start(bf16[4,4,256,64]{2,3,1,0:T(8,128)(2,1)S(1)} %fusion.72), channel_id=1, source_target_pairs={{0,8},{8,16},{16,24},{24,0},{1,9},{9,17},{17,25},{25,1},{2,10},{10... | collective-permute-start | bytes 1572872 | tf_op jit(solution)/shard_map/ppermute | solution.py:22
  654.5 90.2 %copy-start.1 = (bf16[1024,1024]{1,0:T(8,128)(2,1)S(1)}, bf16[1024,1024]{1,0:T(8,128)(2,1)}, u32[]{:S(2)}) copy-start(bf16[1024,1024]{1,0:T(8,128)(2,1)} %param.27) | copy-start | bytes 6291460
  656.3 87.7 %copy-start.26 = (f32[2,64,256]{2,1,0:T(8,128)S(1)}, f32[2,64,256]{2,1,0:T(8,128)}, u32[]{:S(2)}) copy-start(f32[2,64,256]{2,1,0:T(8,128)} %all-reduce.14.cloned.1.call-done) | copy-start | bytes 393220
  (28 other events, 56.3 us)
Sparse Core Ops, SparseCore 0:
  119.7 83.2 all-reduce.5
  225.7 85.6 all-reduce.7
  333.7 85.6 all-reduce.9
  442.2 100.2 all-reduce.13
  653.6 84.4 all-reduce.11
where the time goes:
time: 761 us; the launch traced here: 752 us
  waiting for transfers between devices  506 us (66%)
  matrix products  114 us (15%)
  local copies, waits for them, and re-layouts  51.9 us (7%)
  other arithmetic  37.2 us (5%)
  starting transfers between devices  27.4 us (4%)
  between operations  14.8 us (2%)
    ppermute x25, waiting for transfers between devices, shifted(): return lax.ppermute(value, axis, pairs)  171 us
    psum x1, waiting for transfers between devices, body(): lax.psum(jnp.dot(activated.astype(jnp.bfloat16), w_down, preferred_elemen...  85.7 us
    psum x1, waiting for transfers between devices, body(): grad_normed = grad_two + lax.psum(hidden_part, 'head')  85.5 us
    psum x1, waiting for transfers between devices, body(): lax.psum(jnp.dot(merged, w_out, preferred_element_type=jnp.float32), 'head')  82.6 us
    psum x1, waiting for transfers between devices, body(): input_grad = grad_one + lax.psum(input_part, 'head')  81.7 us
    ppermute x25, starting transfers between devices, shifted(): return lax.ppermute(value, axis, pairs)  26.5 us
    unnamed x74, local copies, waits for them, and re-layouts  15.8 us
    dot_general x4, matrix products, back_block(): jnp.einsum('shqk,shqd->shkd', probabilities.astype(jnp.bfloat16), grad_at...  15.7 us
  transfers between devices with their start and end apart: 30, of which 14 were waited for; matrix products, arithmetic and copies ran while one was open for 12% of the time, Pallas kernels for 0%

commit v1 on v0

--- a/solution.py
+++ b/solution.py
@@ -1,6 +1,8 @@
 import jax
 import jax.numpy as jnp
 from jax import lax
+from jax.experimental import pallas as pl
+from jax.experimental.pallas import tpu as pltpu
 from jax.sharding import PartitionSpec as P
 
 HEAD_DIM = 64
@@ -83,7 +85,7 @@
     return (grad_queries, grad_keys, grad_values)
 
 
-def body(
+def general_body(
     tokens,
     cotangent,
     prefix,
@@ -303,6 +305,573 @@
     )
 
 
+BF = jnp.bfloat16
+F32 = jnp.float32
+MESH = pl.DeviceIdType.MESH
+AHEAD = 3
+
+
+def nn(left, right):
+    return jnp.dot(left, right, preferred_element_type=F32)
+
+
+def nt(left, right):
+    return lax.dot_general(
+        left, right, (((1,), (1,)), ((), ())), preferred_element_type=F32
+    )
+
+
+def remote(src, dst, send, recv, device):
+    return pltpu.make_async_remote_copy(
+        src, dst, send, recv, device_id=device, device_id_type=MESH
+    )
+
+
+def rows_at(start, size, step=64):
+    return pl.ds(pl.multiple_of(start, step), size)
+
+
+def places():
+    z = lax.axis_index("seq")
+    h = lax.axis_index("head")
+    y = lax.axis_index("batch")
+    return z, h, y
+
+
+def member(h, u):
+    chip, core = h // 2, lax.rem(h, 2)
+    return 2 * lax.rem(chip + u // 2, 2) + lax.rem(core + u % 2, 2)
+
+
+def z_peers(z):
+    return [z + 1 - 2 * lax.rem(z, 2), 3 - z, lax.rem(z + 2, 4)]
+
+
+def greet(devices):
+    barrier = pltpu.get_barrier_semaphore()
+    for device in devices:
+        pl.semaphore_signal(barrier, inc=1, device_id=device, device_id_type=MESH)
+    pl.semaphore_wait(barrier, len(devices))
+
+
+def lane_masks():
+    lane = lax.broadcasted_iota(jnp.int32, (1, 128), 1)
+    inside = [lane < HEAD_DIM, lane >= HEAD_DIM]
+    spare = [lane == HEAD_DIM, lane == 0]
+    return inside, spare
+
+
+def front_kernel(
+    tokens,
+    cot,
+    w_qkv,
+    w_out,
+    w_in,
+    w_down,
+    prefix,
+    proj_bias,
+    ffn_bias,
+    gains,
+    shifts,
+    lengths,
+    key_mask,
+    pt_o,
+    q_o,
+    k_o,
+    v_o,
+    rl_o,
+    att_o,
+    lo_o,
+    g1_o,
+    da_o,
+    tok,
+    cotg,
+    bias_s,
+    bias_g,
+    wq,
+    wo,
+    wi,
+    wd,
+    fb,
+    q_s,
+    k_s,
+    v_s,
+    kx,
+    vtx,
+    pt,
+    att_loc,
+    att_all,
+    rl_s,
+    normed_s,
+    xhat_s,
+    nb_s,
+    acc,
+    act,
+    gp,
+    lo_s,
+    da_s,
+    loc_sem,
+    out_sem,
+    pt_sem,
+    tok_sem,
+    cot_sem,
+    bias_sem,
+    fb_sem,
+    att_sem,
+    core_sem,
+    x_sem,
+    y_sem,
+    c1_sem,
+    c2_sem,
+):
+    z, h, y = places()
+    core = lax.rem(h, 2)
+    hc, hx, hd_ = member(h, 1), member(h, 2), member(h, 3)
+    dev_core, dev_x, dev_diag, dev_y = (z, hc, y), (z, hx, y), (z, hd_, y), (z, h, 1 - y)
+    zs = z_peers(z)
+    width = tok.shape[1]
+    piece = width // 4
+    slots = prefix.shape[1]
+    total = 4 * width
+    greet([dev_core, dev_x, dev_diag, dev_y] + [(zp, h, y) for zp in zs])
+
+    half = width // 2
+    my_half = rows_at(core * half, half)
+    tok_copies, tok_forwards = [], []
+    for k, zp in enumerate(zs):
+        tok_copies.append(
+            remote(tokens.at[zp, my_half], tok.at[z, my_half], tok_sem.at[0, k], tok_sem.at[1, k], (zp, h, y))
+        )
+        tok_forwards.append(
+            remote(tok.at[zp, my_half], tok.at[zp, my_half], tok_sem.at[2, k], tok_sem.at[3, k], dev_core)
+        )
+    for copy in tok_copies:
+        copy.start()
+    tok_own = pltpu.make_async_copy(tokens.at[z], tok.at[z], loc_sem.at[0])
+    tok_own.start()
+    wq_own = pltpu.make_async_copy(w_qkv, wq, loc_sem.at[1])
+    wq_own.start()
+
+    chunks = [(w_out, wo, w_out.shape[0] // 2, 0, w_out.shape[0] // 2)]
+    for src, dst in ((w_in, wi), (w_down, wd)):
+        deep = src.shape[0] // 2
+        for i in range(4):
+            chunks.append((src, dst, deep, i * (deep // 4), deep // 4))
+    over_x, over_y, core_x, core_y = [], [], [], []
+    for i, (src, dst, deep, offset, size) in enumerate(chunks):
+        mine = rows_at(y * deep + offset, size, 128)
+        other = rows_at((1 - y) * deep + offset, size, 128)
+        over_x.append(remote(src.at[mine], dst.at[h, mine], x_sem.at[0, i], x_sem.at[1, i], dev_x))
+        over_y.append(remote(dst.at[hx, mine], dst.at[hx, mine], y_sem.at[0, i], y_sem.at[1, i], dev_y))
+        core_x.append(remote(dst.at[hx, mine], dst.at[hx, mine], c1_sem.at[0, i], c1_sem.at[1, i], dev_core))
+        core_y.append(remote(dst.at[hx, other], dst.at[hx, other], c2_sem.at[0, i], c2_sem.at[1, i], dev_core))
+    n_chunks = len(chunks)
+    for copy in over_x[:AHEAD]:
+        copy.start()
+
+    def serve_x(i):
+        over_x[i].wait_recv()
+        over_y[i].start()
+        core_x[i].start()
+        if i + AHEAD < n_chunks:
+            over_x[i + AHEAD].start()
+
+    def serve_y(i):
+        over_y[i].wait_recv()
+        core_y[i].start()
+
+    own_weights, core_weights = [], []
+    for i, (src, dst) in enumerate(((w_out, wo), (w_in, wi), (w_down, wd))):
+        own_weights.append(pltpu.make_async_copy(src, dst.at[h], loc_sem.at[2 + i]))
+        core_weights.append(remote(src, dst.at[h], core_sem.at[0, i], core_sem.at[1, i], dev_core))
+
+    spot = lax.broadcasted_iota(jnp.int32, (8, width), 1) + z * width
+    for s in range(4):
+        live = (jnp.broadcast_to(key_mask[s : s + 1, :], (8, width)) == 1) & (spot < lengths[s])
+        bias_s[s] = jnp.where(live, 0.0, NEG_FILL)
+    bias_g[z] = bias_s[z]
+    bias_copies = [
+        remote(bias_s.at[zp], bias_g.at[z], bias_sem.at[0, k], bias_sem.at[1, k], (zp, h, y))
+        for k, zp in enumerate(zs)
+    ]
+    fb[h] = jnp.broadcast_to(ffn_bias[...], fb.shape[1:])
+    fb_copies = [
+        remote(fb.at[h], fb.at[h], fb_sem.at[0, k], fb_sem.at[1, k], device)
+        for k, device in enumerate((dev_core, dev_x, dev_diag))
+    ]
+    for copy in bias_copies + fb_copies:
+        copy.start()
+    for copy in own_weights + core_weights:
+        copy.start()
+
+    my_piece = rows_at(h * piece, piece)
+    cot_copies = [
+        remote(cot.at[zp, my_piece], cotg.at[z], cot_sem.at[0, k], cot_sem.at[1, k], (zp, h, y))
+        for k, zp in enumerate(zs)
+    ]
+    cot_own = pltpu.make_async_copy(cot.at[z, my_piece], cotg.at[z], loc_sem.at[5])
+    cot_own.start()
+
+    inside, spare = lane_masks()
+
+    pk = prefix[0].astype(BF)
+    pv = prefix[1].astype(BF)
+    k_s[total : total + slots, :] = pk
+    v_s[total : total + slots, :] = pv
+    for head in range(4):
+        pair, par = head // 2, head % 2
+        part = pk[:, 128 * pair : 128 * pair + 128].astype(F32)
+        kx[head, total : total + slots, :] = jnp.where(inside[par], part, 0.0).astype(BF)
+        vtx[head, HEAD_DIM:, :] = jnp.ones((vtx.shape[1] - HEAD_DIM, vtx.shape[2]), BF)
+
+    def project(block):
+        rows = tok[block]
+        for i, target in enumerate((q_s, k_s, v_s)):
+            value = (nn(rows, wq[i]) + proj_bias[i : i + 1, :]).astype(BF)
+            if i == 0:
+                value = (value.astype(F32) * HEAD_DIM**-0.5).astype(BF)
+            for j in range(4):
+                target[rows_at(j * width + block * piece, piece), :] = value[piece * j : piece * j + piece]
+            if i == 1:
+                column = jnp.broadcast_to(bias_g[block][0:1, :], (128, width)).T
+                for head in range(4):
+                    pair, par = head // 2, head % 2
+                    part = value[:, 128 * pair : 128 * pair + 128].astype(F32)
+                    ext = jnp.where(inside[par], part, jnp.where(spare[par], column, 0.0)).astype(BF)
+                    for j in range(4):
+                        kx[head, rows_at(j * width + block * piece, piece), :] = ext[piece * j : piece * j + piece]
+
+    tok_own.wait()
+    wq_own.wait()
+    project(z)
+    serve_x(0)
+    for k, zp in enumerate(zs):
+        serve_x(k + 1)
+        serve_y(k)
+        tok_copies[k].wait_recv()
+        tok_forwards[k].start()
+        bias_copies[k].wait_recv()
+        if k == 0:
+            for copy in cot_copies:
+                copy.start()
+        tok_forwards[k].wait_recv()
+        project(zp)
+
+    for i in range(4):
+        flipped = v_s[i * width : (i + 1) * width, :].astype(F32).T.astype(BF)
+        for head in range(4):
+            vtx[head, 0:HEAD_DIM, i * width : (i + 1) * width] = flipped[HEAD_DIM * head : HEAD_DIM * (head + 1)]
+    flipped = v_s[total : total + slots, :].astype(F32).T.astype(BF)
+    for head in range(4):
+        vtx[head, 0:HEAD_DIM, total : total + slots] = flipped[HEAD_DIM * head : HEAD_DIM * (head + 1)]
+
+    q_out = pltpu.make_async_copy(q_s, q_o, out_sem.at[0])
+    k_out = pltpu.make_async_copy(k_s, k_o, out_sem.at[1])
+    v_out = pltpu.make_async_copy(v_s, v_o, out_sem.at[2])
+    for copy in (q_out, k_out, v_out):
+        copy.start()
+
+    att_copies = []
+    pt_out = []
+    for step in range(4):
+        u = 3 - step
+        j = member(h, u) if u else h
+        outs, recips = [], []
+        for head in range(4):
+            pair, par = head // 2, head % 2
+            part = q_s[rows_at(j * width, width, width), 128 * pair : 128 * pair + 128].astype(F32)
+            ext = jnp.where(inside[par], part, jnp.where(spare[par], 1.0, 0.0)).astype(BF)
+            scores = nt(kx[head], ext)
+            top = jnp.max(scores, axis=0, keepdims=True)
+            weight = jnp.exp(scores - top).astype(BF)
+            pt[head, j] = weight
+            summed = nn(vtx[head], weight)
+            recip = 1.0 / summed[HEAD_DIM : HEAD_DIM + 1]
+            outs.append(summed[0:HEAD_DIM] * recip)
+            recips.append(jnp.broadcast_to(recip, (32, width)))
+            copy = pltpu.make_async_copy(pt.at[head, j], pt_o.at[head, j], pt_sem.at[step, head])
+            copy.start()
+            pt_out.append(copy)
+        att_loc[j] = jnp.concatenate(outs, axis=0).T.astype(BF)
+        rl_s[j] = jnp.concatenate(recips, axis=0).T
+        if u:
+            copy = remote(att_loc.at[j], att_all.at[h], att_sem.at[0, u], att_sem.at[1, u], (z, j, y))
+            copy.start()
+            att_copies.append(copy)
+        else:
+            att_all[h] = att_loc[h]
+        if step < 2:
+            serve_x(4 + step)
+            serve_y(3 + step)
+    rl_out = pltpu.make_async_copy(rl_s, rl_o, out_sem.at[3])
+    att_out = pltpu.make_async_copy(att_loc, att_o, out_sem.at[4])
+    rl_out.start()
+    att_out.start()
+
+    own_weights[0].wait()
+    core_weights[0].wait_recv()
+    core_x[0].wait_recv()
+    core_y[0].wait_recv()
+    for copy in att_copies:
+        copy.wait_recv()
+    attention = nn(att_all[0], wo[0])
+    for j in range(1, 4):
+        attention += nn(att_all[j], wo[j])
+    mine = jnp.concatenate([tok[b, my_piece, :] for b in range(4)], axis=0).astype(F32)
+    resid = mine + attention + shifts[0:1, :]
+    centred = resid - jnp.mean(resid, axis=-1, keepdims=True)
+    inverse_one = lax.rsqrt(jnp.mean(centred * centred, axis=-1, keepdims=True) + NORM_EPSILON)
+    xhat = centred * inverse_one
+    xhat_s[...] = xhat
+    normed = xhat * gains[0:1, :] + shifts[1:2, :]
+    normed_s[...] = normed
+    nb_s[...] = normed.astype(BF)
+
+    tile = 256
+    tiles = wi.shape[2] // tile
+
+    def ffn_in(quarter):
+        @pl.loop(0, tiles)
+        def _(n):
+            cols = rows_at(n * tile, tile, tile)
+            inner = nn(nb_s[...], wi[quarter, :, cols]) + fb[quarter, 0:1, cols]
+            cdf = 0.5 * (1.0 + lax.erf(inner * 0.7071067811865476))
+            act[quarter, :, cols] = (inner * cdf).astype(BF)
+            gp[quarter, :, cols] = cdf + inner * (jnp.exp(-0.5 * inner * inner) * 0.3989422804014327)
+
+    for copy in fb_copies:
+        copy.wait_recv()
+    own_weights[1].wait()
+    core_weights[1].wait_recv()
+    ffn_in(h)
+    ffn_in(hc)
+    serve_x(6)
+    serve_y(5)
+    for i in range(1, 5):
+        core_x[i].wait_recv()
+        core_y[i].wait_recv()
+    ffn_in(hx)
+    ffn_in(hd_)
+
+    acc[...] = jnp.zeros(acc.shape, F32)
+
+    def ffn_out(quarter, start, deep):
+        span = rows_at(start, deep, deep)
+
+        @pl.loop(0, tiles)
+        def _(n):
+            cols = rows_at(n * tile, tile, tile)
+            acc[:, cols] += nn(act[quarter, :, span], wd[quarter, span, cols])
+
+    own_weights[2].wait()
+    core_weights[2].wait_recv()
+    deep = wd.shape[1]
+    ffn_out(h, 0, deep)
+    serve_x(7)
+    serve_y(6)
+    ffn_out(hc, 0, deep)
+    serve_x(8)
+    serve_y(7)
+    for i in range(5, 9):
+        core_x[i].wait_recv()
+    ffn_out(hx, y * (deep // 2), deep // 2)
+    ffn_out(hd_, y * (deep // 2), deep // 2)
+    serve_y(8)
+    ffn_out(hx, (1 - y) * (deep // 2), deep // 2)
+    for i in range(5, 9):
+        core_y[i].wait_recv()
+    ffn_out(hd_, (1 - y) * (deep // 2), deep // 2)
+
+    resid = normed_s[...] + acc[...] + shifts[2:3, :]
+    centred = resid - jnp.mean(resid, axis=-1, keepdims=True)
+    inverse = lax.rsqrt(jnp.mean(centred * centred, axis=-1, keepdims=True) + NORM_EPSILON)
+    xhat = centred * inverse
+    lo_s[...] = (xhat * gains[1:2, :] + shifts[3:4, :]).astype(BF)
+    lo_out = pltpu.make_async_copy(lo_s, lo_o, out_sem.at[5])
+    lo_out.start()
+    cot_own.wait()
+    for copy in cot_copies:
+        copy.wait_recv()
+    dy = jnp.concatenate([cotg[b] for b in range(4)], axis=0).astype(F32) * gains[1:2, :]
+    g_two = inverse * (
+        dy - jnp.mean(dy, axis=-1, keepdims=True) - xhat * jnp.mean(dy * xhat, axis=-1, keepdims=True)
+    )
+    acc[...] = g_two
+    nb_s[...] = g_two.astype(BF)
+
+    @pl.loop(0, 4)
+    def _(quarter):
+        @pl.loop(0, tiles)
+        def _(n):
+            cols = rows_at(n * tile, tile, tile)
+            d_act = nt(nb_s[...], wd[quarter, cols, :])
+            act[quarter, :, cols] = (d_act * gp[quarter, :, cols]).astype(BF)
+
+    @pl.loop(0, 4)
+    def _(quarter):
+        @pl.loop(0, tiles)
+        def _(n):
+            cols = rows_at(n * tile, tile, tile)
+            acc[:, cols] += nt(act[quarter], wi[quarter, cols, :])
+
+    dy = acc[...] * gains[0:1, :]
+    xhat = xhat_s[...]
+    g_one = inverse_one * (
+        dy - jnp.mean(dy, axis=-1, keepdims=True) - xhat * jnp.mean(dy * xhat, axis=-1, keepdims=True)
+    )
+    acc[...] = g_one
+    g1_out = pltpu.make_async_copy(acc, g1_o, out_sem.at[6])
+    g1_out.start()
+    low = g_one.astype(BF)
+    for j in range(4):
+        da_s[j] = nt(low, wo[j]).astype(BF)
+    da_out = pltpu.make_async_copy(da_s, da_o, out_sem.at[7])
+    da_out.start()
+
+    for copy in [q_out, k_out, v_out, rl_out, att_out, lo_out, g1_out, da_out] + pt_out:
+        copy.wait()
+    sent = tok_copies + tok_forwards + over_x + over_y + core_x + core_y + core_weights
+    for copy in sent + bias_copies + fb_copies + cot_copies + att_copies:
+        copy.wait_send()
+
+
+def front(tokens, cot, w_qkv, w_out, w_in, w_down, prefix, proj_bias, ffn_bias, gains, shifts, lengths, key_mask):
+    seqs, width, model = tokens.shape
+    local = w_qkv.shape[2]
+    hidden = w_in.shape[1]
+    slots = prefix.shape[1]
+    total = seqs * width
+    keys = total + slots
+    dma = pltpu.SemaphoreType.DMA
+    hbm = pl.BlockSpec(memory_space=pl.ANY)
+    vmem = pl.BlockSpec(memory_space=pltpu.VMEM)
+    shape = jax.ShapeDtypeStruct
+    return pl.pallas_call(
+        front_kernel,
+        name="front",
+        out_shape=(
+            shape((4, 4, keys, width), BF),
+            shape((total, local), BF),
+            shape((keys, local), BF),
+            shape((keys, local), BF),
+            shape((4, width, 128), F32),
+            shape((4, width, local), BF),
+            shape((width, model), BF),
+            shape((width, model), F32),
+            shape((4, width, local), BF),
+        ),
+        in_specs=[hbm] * 6 + [vmem] * 5 + [pl.BlockSpec(memory_space=pltpu.SMEM), vmem],
+        out_specs=(hbm,) * 9,
+        scratch_shapes=[
+            pltpu.VMEM((4, width, model), BF),
+            pltpu.VMEM((4, width // 4, model), BF),
+            pltpu.VMEM((4, 8, width), F32),
+            pltpu.VMEM((4, 8, width), F32),
+            pltpu.VMEM((3, model, local), BF),
+            pltpu.VMEM((4, local, model), BF),
+            pltpu.VMEM((4, model, hidden), BF),
+            pltpu.VMEM((4, hidden, model), BF),
+            pltpu.VMEM((4, 8, hidden), F32),
+            pltpu.VMEM((total, local), BF),
+            pltpu.VMEM((keys, local), BF),
+            pltpu.VMEM((keys, local), BF),
+            pltpu.VMEM((4, keys, 128), BF),
+            pltpu.VMEM((4, HEAD_DIM + 16, keys), BF),
+            pltpu.VMEM((4, 4, keys, width), BF),
+            pltpu.VMEM((4, width, local), BF),
+            pltpu.VMEM((4, width, local), BF),
+            pltpu.VMEM((4, width, 128), F32),
+            pltpu.VMEM((width, model), F32),
+            pltpu.VMEM((width, model), F32),
+            pltpu.VMEM((width, model), BF),
+            pltpu.VMEM((width, model), F32),
+            pltpu.VMEM((4, width, hidden), BF),
+            pltpu.VMEM((4, width, hidden), F32),
+            pltpu.VMEM((width, model), BF),
+            pltpu.VMEM((4, width, local), BF),
+            dma((6,)),
+            dma((8,)),
+            dma((4, 4)),
+            dma((4, 3)),
+            dma((2, 3)),
+            dma((2, 3)),
+            dma((2, 3)),
+            dma((2, 4)),
+            dma((2, 3)),
+            dma((2, 9)),
+            dma((2, 9)),
+            dma((2, 9)),
+            dma((2, 9)),
+        ],
+        compiler_params=pltpu.CompilerParams(
+            collective_id=0, has_side_effects=True, vmem_limit_bytes=60 * 2**20
+        ),
+        cost_estimate=pl.CostEstimate(flops=15 * 10**9, bytes_accessed=40 * 2**20, transcendentals=6 * 10**6),
+    )(tokens, cot, w_qkv, w_out, w_in, w_down, prefix, proj_bias, ffn_bias, gains, shifts, lengths, key_mask)
+
+
+def back_plain(pt, q, k, v, rl, att, lo, g1, da, w_qkv, prefix_slots):
+    heads = 4
+    total = q.shape[0]
+    width = g1.shape[0]
+    piece = width // 4
+    d_att = lax.all_to_all(da, "head", 0, 0)
+    rows = lambda value: value.reshape(4, width, heads, HEAD_DIM).transpose(2, 0, 1, 3)
+    d_att_h, att_h = rows(d_att), rows(att)
+    q_h = rows(q)
+    k_h = k.reshape(-1, heads, HEAD_DIM).transpose(1, 0, 2)
+    v_h = v.reshape(-1, heads, HEAD_DIM).transpose(1, 0, 2)
+    delta = jnp.sum(d_att_h.astype(F32) * att_h.astype(F32), -1)
+    recip = jnp.stack([rl[:, :, 32 * i] for i in range(heads)])
+    probs = pt.astype(F32) * recip[:, :, None, :]
+    dp = jnp.einsum("hkd,hjrd->hjkr", v_h, d_att_h, preferred_element_type=F32)
+    ds = (probs * (dp - delta[:, :, None, :])).astype(BF)
+    dq = jnp.einsum("hjkr,hkd->hjrd", ds, k_h, preferred_element_type=F32) * HEAD_DIM**-0.5
+    dk = jnp.einsum("hjkr,hjrd->hkd", ds, q_h, preferred_element_type=F32)
+    dv = jnp.einsum("hjkr,hjrd->hkd", probs.astype(BF), d_att_h, preferred_element_type=F32)
+    flat = lambda value: value.transpose(1, 0, 2).reshape(-1, heads * HEAD_DIM)
+    dk, dv = flat(dk), flat(dv)
+    dq = dq.transpose(1, 2, 0, 3).reshape(total, heads * HEAD_DIM)
+    prefix_terms = jnp.stack([dk[total:], dv[total:]])
+    grads = jnp.stack([dq, dk[:total], dv[:total]]).astype(BF)
+    part = jnp.einsum("ite,ide->td", grads, w_qkv, preferred_element_type=F32)
+    own = lax.psum_scatter(part, "head", scatter_dimension=0, tiled=True) + g1
+    both = jnp.stack([own, lo.astype(F32)]).reshape(2, 4, piece, -1)
+    moved = lax.all_to_all(both, "seq", 1, 1)
+    full = lax.all_gather(moved, "head", axis=2, tiled=True)
+    return full[1], full[0], prefix_terms
+
+
+def body(*args):
+    (tokens, cotangent, prefix, first_moment, second_moment, w_qkv, proj_bias, w_out, w_in, ffn_bias) = args[:10]
+    w_down, gains, shifts, lengths, key_mask = args[10:]
+    fits = (
+        lax.axis_size("seq") == 4
+        and lax.axis_size("head") == 4
+        and lax.axis_size("batch") == 2
+        and tokens.shape == (4, 256, 1024)
+        and w_qkv.shape == (3, 1024, 256)
+        and w_in.shape == (1024, 1024)
+        and prefix.shape[1] == 64
+    )
+    if not fits:
+        return general_body(*args)
+    parts = front(
+        tokens, cotangent, w_qkv, w_out, w_in, w_down, prefix, proj_bias, ffn_bias.reshape(1, -1), gains, shifts,
+        lengths, key_mask,
+    )
+    layer_out, input_grad, prefix_terms = back_plain(*parts, w_qkv, prefix.shape[1])
+    prefix_grad = lax.psum(prefix_terms, ("seq", "batch"))
+    new_first = BETA_ONE * first_moment + (1.0 - BETA_ONE) * prefix_grad
+    new_second = BETA_TWO * second_moment + (1.0 - BETA_TWO) * prefix_grad * prefix_grad
+    first_hat = new_first / (1.0 - BETA_ONE**STEP)
+    second_hat = new_second / (1.0 - BETA_TWO**STEP)
+    new_prefix = prefix - LEARN_RATE * (
+        first_hat / (jnp.sqrt(second_hat) + ADAM_EPSILON) + WEIGHT_DECAY * prefix
+    )
+    return layer_out, input_grad, prefix_grad, new_prefix, new_first, new_second
+
+
 def solution(mesh):
     placed = (
         P("batch", "seq", None),

time: 761 us -> 329 us (0.43); the launches traced: 752 us -> 329 us
  waiting for transfers between devices: 506 us -> 146 us
  Pallas kernels: 0 us -> 99.3 us
  matrix products: 114 us -> 26.3 us
  other arithmetic: 37.2 us -> 6.84 us
  local copies, waits for them, and re-layouts: 51.9 us -> 26.3 us
  starting transfers between devices: 27.4 us -> 8.3 us
    psum x4 -> x0, waiting for transfers between devices: 336 us -> none  [the longest x1 85.7 us: body(): lax.psum(jnp.dot(activated.astype(jnp.bfloat16), w_down, preferred_elemen...]
    ppermute x25 -> x0, waiting for transfers between devices: 171 us -> none  [shifted(): return lax.ppermute(value, axis, pairs)]
    pallas_call x0 -> x1, Pallas kernels: none -> 99.3 us  [front(): pl.pallas_call(front_kernel, name='front', out_shape=(shape((4, 4, keys,...]
    dot_general x41 -> x5, matrix products: 114 us -> 26.3 us  [the longest x1 7.39 us: back_plain(): jnp.einsum('hjkr,hjrd->hkd', probs.astype(BF), d_att_h, preferred_element...]
    all_to_all x0 -> x2, waiting for transfers between devices: none -> 49.6 us  [the longest x1 49.1 us: back_plain(): moved = lax.all_to_all(both, 'seq', 1, 1)]
    reduce_scatter x0 -> x1, waiting for transfers between devices: none -> 41.7 us  [back_plain(): own = lax.psum_scatter(part, 'head', scatter_dimension=0, tiled=True) + g1]
    psum x1, waiting for transfers between devices: 0.02 us -> 41.5 us  [body(): prefix_grad = lax.psum(prefix_terms, ('seq', 'batch'))]
    reduce_sum x13 -> x1, other arithmetic: 27.3 us -> 0.16 us  [back_plain(): delta = jnp.sum(d_att_h.astype(F32) * att_h.astype(F32), -1)]
  transfers between devices with their start and end apart: 30 -> 5, of which waited for: 14 -> 5; matrix products, arithmetic and copies ran while one was open for 12% -> 4% of each run, Pallas kernels for 0% -> 0%
where the time goes in v1:
time: 329 us
  waiting for transfers between devices  146 us (44%)
  Pallas kernels  99.3 us (30%)
  local copies, waits for them, and re-layouts  26.3 us (8%)
  matrix products  26.3 us (8%)
  between operations  15.7 us (5%)
  starting transfers between devices  8.3 us (3%)
  other arithmetic  6.84 us (2%)
    pallas_call x1, Pallas kernels, front(): pl.pallas_call(front_kernel, name='front', out_shape=(shape((4, 4, keys,...  99.3 us
    all_to_all x1, waiting for transfers between devices, back_plain(): moved = lax.all_to_all(both, 'seq', 1, 1)  49.1 us
    reduce_scatter x1, waiting for transfers between devices, back_plain(): own = lax.psum_scatter(part, 'head', scatter_dimension=0, tiled=True) + g1  41.7 us
    psum x1, waiting for transfers between devices, body(): prefix_grad = lax.psum(prefix_terms, ('seq', 'batch'))  41.5 us
    all_gather x1, waiting for transfers between devices, back_plain(): full = lax.all_gather(moved, 'head', axis=2, tiled=True)  13.1 us
    squeeze x1, local copies, waits for them, and re-layouts, back_plain(): return (full[1], full[0], prefix_terms)  8.52 us
    dot_general x1, matrix products, back_plain(): jnp.einsum('hjkr,hjrd->hkd', probs.astype(BF), d_att_h, preferred_element...  7.39 us
  transfers between devices with their start and end apart: 5, of which 5 were waited for; matrix products, arithmetic and copies ran while one was open for 4% of the time, Pallas kernels for 0%

profile of v1, /device:TPU:0, one launch (start us, length us, event | category | flops | bytes accessed | tf_op | source)
XLA Modules:
  0.0 328.7 jit_solution(12304798714829726607)
XLA Ops:
  8.0 99.3 %front.1 = (bf16[4,4,1088,256]{3,2,1,0:T(8,128)(2,1)}, bf16[1024,256]{1,0:T(8,128)(2,1)}, bf16[1088,256]{1,0:T(8,128)(2,1)}, bf16[1088,256]{1,0:T(8,128)(2,1)}, ...) custom-call(bf16[4,256,1024]{2,1,0:T(8,128)(2,1)} %tokens.1, ...), custom_call_target="tpu_custom_call" | custom-call | flops 15000000512 | bytes 41943040 | tf_op jit(solution)/shard_map/front/pallas_call | solution.py:749
  107.3 3.6 %all-to-all-start = ((bf16[4,256,256]{2,1,0:T(8,128)(2,1)}), bf16[4,256,256]{2,1,0:T(8,128)(2,1)S(1)}, u32[]{:S(2)}, u32[]{:S(2)}) async-start(bf16[4,256,256]{2,1,0:T(8,128)(2,1)} %get-tuple-element.17), calls=%async_computation | async-start | bytes 1048576 | tf_op jit(solution)/shard_map/all_to_all | solution.py:818
  110.9 0.0 reduce-scatter.2.cloned.1.call-start
  111.0 1.2 copy.95
  112.2 2.1 copy.94
  114.3 1.3 copy.97
  115.7 1.2 copy.99
  116.9 1.2 reshape.52
  118.1 1.1 slice_reduce_fusion.3
  119.2 0.6 all-to-all-done
  119.7 0.2 copy.92
  119.9 0.2 fusion.15
  120.1 0.0 copy-start.5
  120.1 7.4 %fusion.5 = f32[1088,4,64]{0,2,1:T(8,128)} fusion(bf16[4,4,1088,256]{3,2,1,0:T(8,128)(2,1)} %get-tuple-element.15, f32[4,4,256]{2,1,0:T(4,128)S(1)} %pad_maximum_fusion.2, bf16[4,256,4,64]{1,3,2,0:T(8,128)(2,1)S(1)} %bitcast.77), kind=kOutput, calls=%fused_computation.10 | convolution fusion | flops 583794688 | bytes 10567680 | tf_op jit(solution)/shard_map/hjkr,hjrd->hkd/dot_general | solution.py:831
  127.5 0.0 copy-done.5
  127.5 5.5 %fusion = bf16[4,4,1088,256]{3,2,1,0:T(8,128)(2,1)S(1)} fusion(bf16[4,4,1088,256]{3,2,1,0:T(8,128)(2,1)} %get-tuple-element.15, bf16[4,1088,64,1]{1,2,3,0:T(8,128)(2,1)S(1)} %bitcast.82, f32[4,4,256]{2,1,0:T(4,128)S(1)} %fusion.15, f32[4,4,256]{2,1,0:T(4,128)S(1)} %pad_maximum_fusion.2, bf16[4,256,4,64]{1,3,2,0:T(8,128)(2,1)S(1)} %bitcast.78), kind=kOutput, calls=%fused_computation.2 | convolution fusion | flops 592707584 | bytes 18939904 | tf_op jit(solution)/shard_map/hkd,hjrd->hjkr/dot_general | solution.py:827
  133.0 0.0 copy-start
  133.0 3.4 %copy-done = bf16[4,4,1088,256]{3,2,1,0:T(8,128)(2,1)} copy-done((bf16[4,4,1088,256]{3,2,1,0:T(8,128)(2,1)}, bf16[4,4,1088,256]{3,2,1,0:T(8,128)(2,1)S(1)}, u32[]{:S(2)}) %copy-start) | copy-done | bytes 8912920
  136.5 1.7 fusion.14
  138.2 0.7 copy.112
  138.9 0.7 reshape.60
  139.6 6.3 %convolution_bitcast_fusion = f32[1088,4,64]{0,2,1:T(8,128)S(1)} fusion(bf16[4,4,1088,256]{3,2,1,0:T(8,128)(2,1)} %copy-done, bf16[4,4,256,64]{2,1,3,0:T(4,128)(2,1)S(1)} %bitcast.81), kind=kOutput, calls=%fused_computation.9 | convolution fusion | flops 570425344 | bytes 10551296 | tf_op jit(solution)/shard_map/hjkr,hjrd->hkd/dot_general | solution.py:830
  145.8 0.1 slice.61
  145.9 0.2 copy.102
  146.1 1.3 slice.60
  147.4 1.0 copy.103
  148.4 5.4 %convolution_bitcast_fusion.1 = f32[1024,1024]{1,0:T(8,128)} fusion(bf16[3,1024,256]{2,1,0:T(8,128)(2,1)} %w_qkv.1, bf16[1,1024,256]{2,1,0:T(8,128)(2,1)} %copy.103, bf16[1,1024,256]{2,1,0:T(8,128)(2,1)S(1)} %copy.102, bf16[1,1024,256]{2,1,0:T(8,128)(2,1)S(1)} %reshape.60), kind=kOutput, calls=%fused_computation.11 | convolution fusion | flops 1612185600 | bytes 7340032 | tf_op jit(solution)/shard_map/ite,ide->td/dot_general | solution.py:837
  153.8 0.0 reduce-scatter.2.cloned.1.call-update
  153.9 1.2 convert.22
  155.1 41.7 %reduce-scatter.2.cloned.1.call-done = f32[256,1024]{1,0:T(8,128)} async-done(((f32[1024,1024]{1,0:T(8,128)}), f32[256,1024]{1,0:T(8,128)}) %reduce-scatter.2.cloned.1.call-update) | async-done | bytes 1048592 | tf_op jit(solution)/shard_map/reduce_scatter | solution.py:838
  196.8 1.4 add.22
  198.1 0.0 slice-start
  198.2 1.5 pad_maximum_fusion
  199.7 4.6 %all-to-all-start.1 = ((f32[2,4,64,1024]{3,2,0,1:T(8,128)}), f32[2,4,64,1024]{3,2,0,1:T(8,128)S(1)}, u32[]{:S(2)}, u32[]{:S(2)}) async-start(f32[2,4,64,1024]{3,2,0,1:T(8,128)} %pad_maximum_fusion), calls=%async_computation.2 | async-start | bytes 4194304 | tf_op jit(solution)/shard_map/all_to_all | solution.py:840
  204.3 0.0 all-reduce.2.cloned.1.call-start
  204.3 0.1 copy.106
  204.4 0.1 copy.107
  204.5 0.7 pad_maximum_fusion.1
  205.2 0.0 all-reduce.2.cloned.1.call-update
  205.2 0.0 all-gather.2.cloned.1.call-start
  205.2 49.1 %all-to-all-done.1 = f32[2,4,64,1024]{3,2,0,1:T(8,128)S(1)} async-done(((f32[2,4,64,1024]{3,2,0,1:T(8,128)}), f32[2,4,64,1024]{3,2,0,1:T(8,128)S(1)}, u32[]{:S(2)}, u32[]{:S(2)}) %all-to-all-start.1) | async-done | bytes 2097184 | tf_op jit(solution)/shard_map/all_to_all | solution.py:840
  254.3 1.3 copy-done.1
  255.6 0.0 all-gather.2.cloned.1.call-update
  255.6 41.5 %all-reduce.2.cloned.1.call-done = f32[2,64,256]{2,1,0:T(8,128)} async-done(((f32[2,64,256]{2,1,0:T(8,128)}), f32[2,64,256]{2,1,0:T(8,128)}) %all-reduce.2.cloned.1.call-update) | async-done | bytes 131088 | tf_op jit(solution)/shard_map/psum | solution.py:864
  297.1 1.9 multiply_subtract_fusion
  299.0 13.1 %all-gather.2.cloned.1.call-done = f32[2,4,256,1024]{3,2,0,1:T(8,128)} async-done(((f32[2,4,64,1024]{3,2,0,1:T(8,128)}), f32[2,4,256,1024]{3,2,0,1:T(8,128)}) %all-gather.2.cloned.1.call-update) | async-done | bytes 8388624 | tf_op jit(solution)/shard_map/all_gather | solution.py:841
  312.1 8.5 %slice_bitcast_fusion = (f32[4,256,1024]{2,1,0:T(8,128)}, f32[4,256,1024]{2,1,0:T(8,128)}) fusion(f32[2,4,256,1024]{3,2,0,1:T(8,128)} %all-gather.2.cloned.1.call-done), kind=kLoop, calls=%fused_computation.7 | loop fusion | bytes 16777216 | tf_op jit(solution)/shard_map/squeeze | solution.py:842
  320.6 0.7 copy.127
  (12 shorter events, 0.0 us)
Async XLA Ops:
  107.3 10.8 %copy-start.2 = (f32[4,256,128]{2,1,0:T(8,128)S(1)}, f32[4,256,128]{2,1,0:T(8,128)}, u32[]{:S(2)}) copy-start(f32[4,256,128]{2,1,0:T(8,128)} %get-tuple-element.16) | copy-start | bytes 1572868
  107.3 12.4 %all-to-all-start = ((bf16[4,256,256]{2,1,0:T(8,128)(2,1)}), bf16[4,256,256]{2,1,0:T(8,128)(2,1)S(1)}, u32[]{:S(2)}, u32[]{:S(2)}) async-start(bf16[4,256,256]{2,1,0:T(8,128)(2,1)} %get-tuple-element.17), calls=%async_computation | async-start | bytes 1048576 | tf_op jit(solution)/shard_map/all_to_all | solution.py:818
  110.9 85.9 %reduce-scatter.2.cloned.1.call-start = ((), (), s32[]{:S(2)}) async-start(), calls=%async_computation.3 | async-start | bytes 5242880 | tf_op jit(solution)/shard_map/reduce_scatter | solution.py:838
  120.1 7.4 %copy-start.5 = (bf16[1088,256]{0,1:T(8,128)(2,1)S(1)}, bf16[1088,256]{0,1:T(8,128)(2,1)}, u32[]{:S(2)}) copy-start(bf16[1088,256]{0,1:T(8,128)(2,1)} %copy.94) | copy-start | bytes 1671172
  133.0 3.4 %copy-start = (bf16[4,4,1088,256]{3,2,1,0:T(8,128)(2,1)}, bf16[4,4,1088,256]{3,2,1,0:T(8,128)(2,1)S(1)}, u32[]{:S(2)}) copy-start(bf16[4,4,1088,256]{3,2,1,0:T(8,128)(2,1)S(1)} %fusion) | copy-start | bytes 26738692
  136.5 3.1 copy-start.3
  153.8 43.0 %copy-start.4 = (f32[256,1024]{1,0:T(8,128)S(1)}, f32[256,1024]{1,0:T(8,128)}, u32[]{:S(2)}) copy-start(f32[256,1024]{1,0:T(8,128)} %get-tuple-element.22) | copy-start | bytes 3145732
  198.1 6.2 %slice-start = ((f32[1088,4,64]{0,2,1:T(8,128)}), f32[64,4,64]{0,2,1:T(8,128)S(1)}, s32[]{:S(2)}) async-start(f32[1088,4,64]{0,2,1:T(8,128)} %fusion.5), calls=%async_computation.6 | async-start | bytes 262144 | tf_op jit(solution)/shard_map/slice | solution.py:835
  199.7 54.6 %all-to-all-start.1 = ((f32[2,4,64,1024]{3,2,0,1:T(8,128)}), f32[2,4,64,1024]{3,2,0,1:T(8,128)S(1)}, u32[]{:S(2)}, u32[]{:S(2)}) async-start(f32[2,4,64,1024]{3,2,0,1:T(8,128)} %pad_maximum_fusion), calls=%async_computation.2 | async-start | bytes 4194304 | tf_op jit(solution)/shard_map/all_to_all | solution.py:840
  204.3 92.9 %all-reduce.2.cloned.1.call-start = ((), (), s32[]{:S(2)}) async-start(), calls=%async_computation.5 | async-start | bytes 262144 | tf_op jit(solution)/shard_map/psum | solution.py:864
  205.2 106.9 %all-gather.2.cloned.1.call-start = ((), (), s32[]{:S(2)}) async-start(), calls=%async_computation.4 | async-start | bytes 10485760 | tf_op jit(solution)/shard_map/all_gather | solution.py:841
  254.3 1.3 copy-start.1
  299.0 21.6 %copy-start.6 = (f32[2,64,256]{2,1,0:T(8,128)S(1)}, f32[2,64,256]{2,1,0:T(8,128)}, u32[]{:S(2)}) copy-start(f32[2,64,256]{2,1,0:T(8,128)} %all-reduce.2.cloned.1.call-done) | copy-start | bytes 393220
Sparse Core Ops, SparseCore 0:
  154.0 42.7 reduce-scatter.1
  255.7 56.2 all-gather.1
Sparse Core Ops, SparseCore 1:
  209.0 88.1 all-reduce.1

commit v2 on v1

--- a/solution.py
+++ b/solution.py
@@ -381,7 +381,8 @@
     v_o,
     rl_o,
     att_o,
-    lo_o,
+    loz_o,
+    lox_o,
     g1_o,
     da_o,
     tok,
@@ -423,6 +424,7 @@
     y_sem,
     c1_sem,
     c2_sem,
+    lo_sem,
 ):
     z, h, y = places()
     core = lax.rem(h, 2)
@@ -687,8 +689,16 @@
     inverse = lax.rsqrt(jnp.mean(centred * centred, axis=-1, keepdims=True) + NORM_EPSILON)
     xhat = centred * inverse
     lo_s[...] = (xhat * gains[1:2, :] + shifts[3:4, :]).astype(BF)
-    lo_out = pltpu.make_async_copy(lo_s, lo_o, out_sem.at[5])
-    lo_out.start()
+    lo_copies = []
+    for k, zp in enumerate(zs):
+        block = rows_at(zp * piece, piece)
+        lo_copies.append(remote(lo_s.at[block], loz_o.at[z], lo_sem.at[0, k], lo_sem.at[1, k], (zp, h, y)))
+    for b in range(4):
+        block = pl.ds(b * piece, piece)
+        lo_copies.append(remote(lo_s.at[block], lox_o.at[b], lo_sem.at[0, 3 + b], lo_sem.at[1, 3 + b], dev_x))
+    lo_out = pltpu.make_async_copy(lo_s.at[rows_at(z * piece, piece)], loz_o.at[z], out_sem.at[5])
+    for copy in lo_copies + [lo_out]:
+        copy.start()
     cot_own.wait()
     for copy in cot_copies:
         copy.wait_recv()
@@ -729,6 +739,8 @@
     da_out.start()
 
     for copy in [q_out, k_out, v_out, rl_out, att_out, lo_out, g1_out, da_out] + pt_out:
+        copy.wait()
+    for copy in lo_copies:
         copy.wait()
     sent = tok_copies + tok_forwards + over_x + over_y + core_x + core_y + core_weights
     for copy in sent + bias_copies + fb_copies + cot_copies + att_copies:
@@ -756,12 +768,13 @@
             shape((keys, local), BF),
             shape((4, width, 128), F32),
             shape((4, width, local), BF),
-            shape((width, model), BF),
+            shape((4, width // 4, model), BF),
+            shape((4, width // 4, model), BF),
             shape((width, model), F32),
             shape((4, width, local), BF),
         ),
         in_specs=[hbm] * 6 + [vmem] * 5 + [pl.BlockSpec(memory_space=pltpu.SMEM), vmem],
-        out_specs=(hbm,) * 9,
+        out_specs=(hbm,) * 10,
         scratch_shapes=[
             pltpu.VMEM((4, width, model), BF),
             pltpu.VMEM((4, width // 4, model), BF),
@@ -802,6 +815,7 @@
             dma((2, 9)),
             dma((2, 9)),
             dma((2, 9)),
+            dma((2, 7)),
         ],
         compiler_params=pltpu.CompilerParams(
             collective_id=0, has_side_effects=True, vmem_limit_bytes=60 * 2**20
@@ -810,36 +824,350 @@
     )(tokens, cot, w_qkv, w_out, w_in, w_down, prefix, proj_bias, ffn_bias, gains, shifts, lengths, key_mask)
 
 
-def back_plain(pt, q, k, v, rl, att, lo, g1, da, w_qkv, prefix_slots):
-    heads = 4
-    total = q.shape[0]
-    width = g1.shape[0]
+def back_kernel(
+    pt_i,
+    q_i,
+    k_i,
+    v_i,
+    rl_i,
+    att_i,
+    loz_i,
+    lox_i,
+    g1_i,
+    da_i,
+    w_qkv,
+    lo_o,
+    ig_o,
+    pre_o,
+    pt,
+    ds,
+    q_s,
+    k_s,
+    v_s,
+    rl_s,
+    att_s,
+    g1_s,
+    wq,
+    da_all,
+    vx,
+    kt,
+    dox,
+    dq_s,
+    core_out,
+    core_in,
+    x_out,
+    x_in,
+    fin,
+    pre_part,
+    pre_land,
+    pre_sum,
+    loc_sem,
+    pt_sem,
+    da_sem,
+    loz_sem,
+    loc2_sem,
+    lo_core_sem,
+    part_core_sem,
+    part_x_sem,
+    igz_sem,
+    igx_sem,
+    igc_sem,
+    igcx_sem,
+    pre_sem,
+    pre2_sem,
+):
+    z, h, y = places()
+    hc, hx, hd_ = member(h, 1), member(h, 2), member(h, 3)
+    dev_core, dev_x, dev_diag = (z, hc, y), (z, hx, y), (z, hd_, y)
+    zs = z_peers(z)
+    width = g1_s.shape[0]
     piece = width // 4
-    d_att = lax.all_to_all(da, "head", 0, 0)
-    rows = lambda value: value.reshape(4, width, heads, HEAD_DIM).transpose(2, 0, 1, 3)
-    d_att_h, att_h = rows(d_att), rows(att)
-    q_h = rows(q)
-    k_h = k.reshape(-1, heads, HEAD_DIM).transpose(1, 0, 2)
-    v_h = v.reshape(-1, heads, HEAD_DIM).transpose(1, 0, 2)
-    delta = jnp.sum(d_att_h.astype(F32) * att_h.astype(F32), -1)
-    recip = jnp.stack([rl[:, :, 32 * i] for i in range(heads)])
-    probs = pt.astype(F32) * recip[:, :, None, :]
-    dp = jnp.einsum("hkd,hjrd->hjkr", v_h, d_att_h, preferred_element_type=F32)
-    ds = (probs * (dp - delta[:, :, None, :])).astype(BF)
-    dq = jnp.einsum("hjkr,hkd->hjrd", ds, k_h, preferred_element_type=F32) * HEAD_DIM**-0.5
-    dk = jnp.einsum("hjkr,hjrd->hkd", ds, q_h, preferred_element_type=F32)
-    dv = jnp.einsum("hjkr,hjrd->hkd", probs.astype(BF), d_att_h, preferred_element_type=F32)
-    flat = lambda value: value.transpose(1, 0, 2).reshape(-1, heads * HEAD_DIM)
-    dk, dv = flat(dk), flat(dv)
-    dq = dq.transpose(1, 2, 0, 3).reshape(total, heads * HEAD_DIM)
-    prefix_terms = jnp.stack([dk[total:], dv[total:]])
-    grads = jnp.stack([dq, dk[:total], dv[:total]]).astype(BF)
-    part = jnp.einsum("ite,ide->td", grads, w_qkv, preferred_element_type=F32)
-    own = lax.psum_scatter(part, "head", scatter_dimension=0, tiled=True) + g1
-    both = jnp.stack([own, lo.astype(F32)]).reshape(2, 4, piece, -1)
-    moved = lax.all_to_all(both, "seq", 1, 1)
-    full = lax.all_gather(moved, "head", axis=2, tiled=True)
-    return full[1], full[0], prefix_terms
+    slots = pre_part.shape[1]
+    total = 4 * width
+    group = 2 * z + y
+    others = [lax.rem(group + d, 8) for d in range(1, 8)]
+    greet([dev_core, dev_x, dev_diag] + [(g // 2, h, lax.rem(g, 2)) for g in others])
+
+    my_piece = rows_at(h * piece, piece)
+    x_piece = rows_at(hx * piece, piece)
+
+    da_copies = []
+    for u in (2, 3, 1):
+        j = member(h, u)
+        da_copies.append(remote(da_i.at[j], da_all.at[h], da_sem.at[0, u], da_sem.at[1, u], (z, j, y)))
+    for copy in da_copies:
+        copy.start()
+    da_wait = {2: da_copies[0], 3: da_copies[1], 1: da_copies[2]}
+
+    loads = []
+    for i, (src, dst) in enumerate(
+        ((da_i.at[h], da_all.at[h]), (v_i, v_s), (k_i, k_s), (rl_i, rl_s), (att_i, att_s), (q_i, q_s), (w_qkv, wq), (g1_i, g1_s))
+    ):
+        loads.append(pltpu.make_async_copy(src, dst, loc_sem.at[i]))
+    for copy in loads[:5]:
+        copy.start()
+    order = [h, hc, hx, hd_]
+    pt_loads = []
+    for u, j in enumerate(order):
+        copy = pltpu.make_async_copy(pt_i.at[:, j], pt.at[:, j], pt_sem.at[u])
+        copy.start()
+        pt_loads.append(copy)
+    for copy in loads[5:]:
+        copy.start()
+
+    loz_copies, lo_forwards = [], []
+    for k, zp in enumerate(zs):
+        loz_copies.append(remote(lox_i.at[zp], lo_o.at[z, x_piece], loz_sem.at[0, k], loz_sem.at[1, k], (zp, h, y)))
+        lo_forwards.append(
+            remote(lo_o.at[zp, x_piece], lo_o.at[zp, x_piece], lo_core_sem.at[0, k], lo_core_sem.at[1, k], dev_core)
+        )
+    for copy in loz_copies:
+        copy.start()
+    lo_local = [
+        pltpu.make_async_copy(loz_i, lo_o.at[:, my_piece], loc2_sem.at[0]),
+        pltpu.make_async_copy(lox_i.at[z], lo_o.at[z, x_piece], loc2_sem.at[1]),
+    ]
+    lo_core = [
+        remote(loz_i, lo_o.at[:, my_piece], lo_core_sem.at[0, 3], lo_core_sem.at[1, 3], dev_core),
+        remote(lox_i.at[z], lo_o.at[z, x_piece], lo_core_sem.at[0, 4], lo_core_sem.at[1, 4], dev_core),
+    ]
+    for copy in lo_local + lo_core:
+        copy.start()
+
+    lane = lax.broadcasted_iota(jnp.int32, (1, 128), 1)
+    inside = [lane < HEAD_DIM, lane >= HEAD_DIM]
+    spare_hi = [lane == HEAD_DIM, lane == 0]
+    spare_lo = [lane == HEAD_DIM + 1, lane == 1]
+
+    loads[1].wait()
+    for head in range(4):
+        pair, par = head // 2, head % 2
+        part = v_s[:, 128 * pair : 128 * pair + 128].astype(F32)
+        ones = jnp.where(spare_hi[par] | spare_lo[par], 1.0, 0.0)
+        vx[head] = jnp.where(inside[par], part, ones).astype(BF)
+    loads[2].wait()
+    for i in range(5):
+        low, size = i * width, width if i < 4 else slots
+        flipped = k_s[low : low + size, :].astype(F32).T.astype(BF)
+        for head in range(4):
+            kt[head, :, low : low + size] = flipped[HEAD_DIM * head : HEAD_DIM * (head + 1)]
+    loads[0].wait()
+    loads[3].wait()
+    loads[4].wait()
+
+    for u, j in enumerate(order):
+        if u:
+            da_wait[u].wait_recv()
+        pt_loads[u].wait()
+        grads = []
+        for head in range(4):
+            pair, par = head // 2, head % 2
+            lanes = slice(128 * pair, 128 * pair + 128)
+            d_out = da_all[j, :, lanes].astype(F32)
+            recip = rl_s[j, :, 32 * head : 32 * head + 1]
+            delta = recip * jnp.sum(
+                jnp.where(inside[par], d_out * att_s[j, :, lanes].astype(F32), 0.0), axis=-1, keepdims=True
+            )
+            high = delta.astype(BF).astype(F32)
+            ext = jnp.where(spare_hi[par], -high, jnp.where(spare_lo[par], high - delta, 0.0))
+            ext = jnp.where(inside[par], d_out * recip, ext).astype(BF)
+            dox[head, j] = ext
+            d_probs = nt(vx[head], ext).astype(BF)
+            d_scores = pt[head, j] * d_probs
+            ds[head, j] = d_scores
+            grads.append(nn(kt[head], d_scores))
+        dq_s[j] = (jnp.concatenate(grads, axis=0).T * HEAD_DIM**-0.5).astype(BF)
+        if u >= 1:
+            loz_copies[u - 1].wait_recv()
+            lo_forwards[u - 1].start()
+
+    def key_side(rows, source, right):
+        halves = []
+        for pair in range(2):
+            sides = []
+            for par in range(2):
+                head = 2 * pair + par
+                value = nn(source[head, 0, rows, :], right(head, 0, pair))
+                for j in range(1, 4):
+                    value += nn(source[head, j, rows, :], right(head, j, pair))
+                sides.append(value)
+            halves.append(jnp.where(inside[0], sides[0], sides[1]))
+        return jnp.concatenate(halves, axis=-1)
+
+    def d_values(rows):
+        return key_side(rows, pt, lambda head, j, pair: dox[head, j])
+
+    def d_keys(rows):
+        return key_side(
+            rows, ds, lambda head, j, pair: q_s[j * width : (j + 1) * width, 128 * pair : 128 * pair + 128]
+        )
+
+    for copy in loads[5:]:
+        copy.wait()
+
+    def partial(i):
+        rows = rows_at(i * width, width, width)
+        dk = d_keys(rows).astype(BF)
+        dv = d_values(rows).astype(BF)
+        return nt(dq_s[i], wq[0]) + nt(dk, wq[1]) + nt(dv, wq[2])
+
+    part_core = [
+        remote(core_out.at[i], core_in.at[i], part_core_sem.at[0, i], part_core_sem.at[1, i], dev_core) for i in range(2)
+    ]
+    blocks = zs + [z]
+    part_x = []
+    for k, b in enumerate(blocks):
+        rows = rows_at(b * piece, piece)
+        part_x.append(remote(x_out.at[rows], x_in.at[rows], part_x_sem.at[0, k], part_x_sem.at[1, k], dev_x))
+
+    core_out[0] = partial(hd_).astype(BF)
+    part_core[0].start()
+    mine = partial(hx)
+    part_core[0].wait_recv()
+    x_out[...] = (mine + core_in[0].astype(F32)).astype(BF)
+    for copy in part_x:
+        copy.start()
+
+    edge = pl.ds(total, slots)
+    pre_part[0] = d_keys(edge)
+    pre_part[1] = d_values(edge)
+    few = slots // 8
+    pre_copies, pre_back = [], []
+    for d, g in enumerate(others):
+        device = (g // 2, h, lax.rem(g, 2))
+        pre_copies.append(
+            remote(pre_part.at[:, rows_at(g * few, few, few)], pre_land.at[d], pre_sem.at[0, d], pre_sem.at[1, d], device)
+        )
+        mine_rows = rows_at(group * few, few, few)
+        pre_back.append(
+            remote(pre_sum.at[:, mine_rows], pre_sum.at[:, mine_rows], pre2_sem.at[0, d], pre2_sem.at[1, d], device)
+        )
+    for copy in pre_copies:
+        copy.start()
+
+    core_out[1] = partial(hc).astype(BF)
+    part_core[1].start()
+    g1_s[...] += partial(h)
+    part_core[1].wait_recv()
+    g1_s[...] += core_in[1].astype(F32)
+
+    igz, igx, igc, igcx = [], [], [], []
+    for k, b in enumerate(blocks):
+        rows = rows_at(b * piece, piece)
+        source = ig_o.at[b, my_piece]
+        if k < 3:
+            igz.append(remote(fin.at[rows], ig_o.at[z, my_piece], igz_sem.at[0, k], igz_sem.at[1, k], (b, h, y)))
+        else:
+            source = fin.at[rows]
+        igx.append(remote(source, ig_o.at[b, my_piece], igx_sem.at[0, k], igx_sem.at[1, k], dev_x))
+        igc.append(remote(source, ig_o.at[b, my_piece], igc_sem.at[0, k], igc_sem.at[1, k], dev_core))
+        igcx.append(
+            remote(ig_o.at[b, x_piece], ig_o.at[b, x_piece], igcx_sem.at[0, k], igcx_sem.at[1, k], dev_core)
+        )
+    ig_local = pltpu.make_async_copy(fin.at[rows_at(z * piece, piece)], ig_o.at[z, my_piece], loc2_sem.at[2])
+    for k, b in enumerate(blocks):
+        rows = rows_at(b * piece, piece)
+        part_x[k].wait_recv()
+        fin[rows, :] = (g1_s[rows, :] + x_in[rows, :].astype(F32)).astype(BF)
+        if k < 3:
+            igz[k].start()
+        else:
+            ig_local.start()
+        if k == 1:
+            for copy in pre_copies:
+                copy.wait_recv()
+            mine_rows = rows_at(group * few, few, few)
+            for i in range(2):
+                term = pre_part[i, mine_rows, :]
+                for d in range(7):
+                    term += pre_land[d, i]
+                pre_sum[i, mine_rows, :] = term
+            for copy in pre_back:
+                copy.start()
+    for k in range(3):
+        igz[k].wait_recv()
+        igx[k].start()
+        igc[k].start()
+        if k == 0:
+            igx[3].start()
+            igc[3].start()
+    for copy in pre_back:
+        copy.wait_recv()
+    pre_o[...] = pre_sum[...]
+    for k in (0, 3, 1, 2):
+        igx[k].wait_recv()
+        igcx[k].start()
+    for copy in igc + igcx + lo_forwards + lo_core:
+        copy.wait_recv()
+    for copy in lo_local + [ig_local]:
+        copy.wait()
+    sent = da_copies + loz_copies + lo_forwards + lo_core + part_core + part_x + igz + igx + igc + igcx
+    for copy in sent + pre_copies + pre_back:
+        copy.wait_send()
+
+
+def back(pt, q, k, v, rl, att, loz, lox, g1, da, w_qkv):
+    width, model = g1.shape
+    keys, local = k.shape
+    total = 4 * width
+    slots = keys - total
+    dma = pltpu.SemaphoreType.DMA
+    hbm = pl.BlockSpec(memory_space=pl.ANY)
+    vmem = pl.BlockSpec(memory_space=pltpu.VMEM)
+    shape = jax.ShapeDtypeStruct
+    return pl.pallas_call(
+        back_kernel,
+        name="back",
+        out_shape=(
+            shape((4, width, model), BF),
+            shape((4, width, model), BF),
+            shape((2, slots, local), F32),
+        ),
+        in_specs=[hbm] * 11,
+        out_specs=(hbm, hbm, vmem),
+        scratch_shapes=[
+            pltpu.VMEM((4, 4, keys, width), BF),
+            pltpu.VMEM((4, 4, keys, width), BF),
+            pltpu.VMEM((total, local), BF),
+            pltpu.VMEM((keys, local), BF),
+            pltpu.VMEM((keys, local), BF),
+            pltpu.VMEM((4, width, 128), F32),
+            pltpu.VMEM((4, width, local), BF),
+            pltpu.VMEM((width, model), F32),
+            pltpu.VMEM((3, model, local), BF),
+            pltpu.VMEM((4, width, local), BF),
+            pltpu.VMEM((4, keys, 128), BF),
+            pltpu.VMEM((4, HEAD_DIM, keys), BF),
+            pltpu.VMEM((4, 4, width, 128), BF),
+            pltpu.VMEM((4, width, local), BF),
+            pltpu.VMEM((2, width, model), BF),
+            pltpu.VMEM((2, width, model), BF),
+            pltpu.VMEM((width, model), BF),
+            pltpu.VMEM((width, model), BF),
+            pltpu.VMEM((width, model), BF),
+            pltpu.VMEM((2, slots, local), F32),
+            pltpu.VMEM((7, 2, slots // 8, local), F32),
+            pltpu.VMEM((2, slots, local), F32),
+            dma((8,)),
+            dma((4,)),
+            dma((2, 4)),
+            dma((2, 3)),
+            dma((3,)),
+            dma((2, 5)),
+            dma((2, 2)),
+            dma((2, 4)),
+            dma((2, 3)),
+            dma((2, 4)),
+            dma((2, 4)),
+            dma((2, 4)),
+            dma((2, 7)),
+            dma((2, 7)),
+        ],
+        compiler_params=pltpu.CompilerParams(
+            collective_id=1, has_side_effects=True, vmem_limit_bytes=60 * 2**20
+        ),
+        cost_estimate=pl.CostEstimate(flops=8 * 10**9, bytes_accessed=30 * 2**20, transcendentals=0),
+    )(pt, q, k, v, rl, att, loz, lox, g1, da, w_qkv)
 
 
 def body(*args):
@@ -860,8 +1188,8 @@
         tokens, cotangent, w_qkv, w_out, w_in, w_down, prefix, proj_bias, ffn_bias.reshape(1, -1), gains, shifts,
         lengths, key_mask,
     )
-    layer_out, input_grad, prefix_terms = back_plain(*parts, w_qkv, prefix.shape[1])
-    prefix_grad = lax.psum(prefix_terms, ("seq", "batch"))
+    layer_out, input_grad, prefix_grad = back(*parts, w_qkv)
+    layer_out, input_grad = layer_out.astype(F32), input_grad.astype(F32)
     new_first = BETA_ONE * first_moment + (1.0 - BETA_ONE) * prefix_grad
     new_second = BETA_TWO * second_moment + (1.0 - BETA_TWO) * prefix_grad * prefix_grad
     first_hat = new_first / (1.0 - BETA_ONE**STEP)

time: 329 us -> 158 us (0.48)
  waiting for transfers between devices: 146 us -> 0 us
  Pallas kernels: 99.3 us -> 149 us
  matrix products: 26.3 us -> 0 us
  local copies, waits for them, and re-layouts: 26.3 us -> 0.68 us
  between operations: 15.7 us -> 0.7 us
  starting transfers between devices: 8.3 us -> 0 us
    all_to_all x2 -> x0, waiting for transfers between devices: 49.6 us -> none  [the longest x1 49.1 us: back_plain(): moved = lax.all_to_all(both, 'seq', 1, 1)]
    pallas_call x0 -> x1, Pallas kernels: none -> 48.8 us  [back(): pl.pallas_call(back_kernel, name='back', out_shape=(shape((4, width, mode...]
    reduce_scatter x1 -> x0, waiting for transfers between devices: 41.7 us -> none  [back_plain(): own = lax.psum_scatter(part, 'head', scatter_dimension=0, tiled=True) + g1]
    psum x1 -> x0, waiting for transfers between devices: 41.5 us -> none  [body(): prefix_grad = lax.psum(prefix_terms, ('seq', 'batch'))]
    dot_general x5 -> x0, matrix products: 26.3 us -> none  [the longest x1 7.39 us: back_plain(): jnp.einsum('hjkr,hjrd->hkd', probs.astype(BF), d_att_h, preferred_element...]
    all_gather x1 -> x0, waiting for transfers between devices: 13.1 us -> none  [back_plain(): full = lax.all_gather(moved, 'head', axis=2, tiled=True)]
    squeeze x1 -> x0, local copies, waits for them, and re-layouts: 8.52 us -> none  [back_plain(): return (full[1], full[0], prefix_terms)]
    all_to_all x2 -> x0, starting transfers between devices: 8.21 us -> none  [the longest x1 4.6 us: back_plain(): moved = lax.all_to_all(both, 'seq', 1, 1)]
  transfers between devices with their start and end apart: 5 -> 0, of which waited for: 5 -> 0; matrix products, arithmetic and copies ran while one was open for 4% -> 0% of each run, Pallas kernels for 0% -> 0%
where the time goes in v2:
time: 158 us
  Pallas kernels  149 us (94%)
  other arithmetic  8.41 us (5%)
    pallas_call x1, Pallas kernels, front(): pl.pallas_call(front_kernel, name='front', out_shape=(shape((4, 4, keys,...  99.8 us
    pallas_call x1, Pallas kernels, back(): pl.pallas_call(back_kernel, name='back', out_shape=(shape((4, width, mode...  48.8 us
    convert_element_type x2, other arithmetic, body(): layer_out, input_grad = (layer_out.astype(F32), input_grad.astype(F32))  6.7 us

profile of v2, /device:TPU:0, one launch (start us, length us, event | category | flops | bytes accessed | tf_op | source)
XLA Modules:
  0.0 158.3 jit_solution(10334426956568486359)
XLA Ops:
  0.6 99.8 %front.1 = (bf16[4,4,1088,256]{3,2,1,0:T(8,128)(2,1)}, bf16[1024,256]{1,0:T(8,128)(2,1)}, bf16[1088,256]{1,0:T(8,128)(2,1)}, bf16[1088,256]{1,0:T(8,128)(2,1)}, ...) custom-call(bf16[4,256,1024]{2,1,0:T(8,128)(2,1)} %tokens.1, ...), custom_call_target="tpu_custom_call" | custom-call | flops 15000000512 | bytes 41943040 | tf_op jit(solution)/shard_map/front/pallas_call | solution.py:761
  100.4 0.0 copy-start.2
  100.4 0.0 copy-start.3
  100.4 0.0 copy-start.4
  100.4 48.8 %back.1 = (bf16[4,256,1024]{2,1,0:T(8,128)(2,1)}, bf16[4,256,1024]{2,1,0:T(8,128)(2,1)}, f32[2,64,256]{2,1,0:T(8,128)}) custom-call(bf16[4,4,1088,256]{3,2,1,0:T(8,128)(2,1)} %get-tuple-element.19.pt_i, bf16[1024,256]{1,0:T(8,128)(2,1)} %get-tuple-element.20.q_i, bf16[1088,256]{1,0:T(8,128)(2,1)} %get-tuple-element.21.k_i, ...), custom_call_target="tpu_custom_call" | custom-call | flops 8000000000 | bytes 31457280 | tf_op jit(solution)/shard_map/back/pallas_call | solution.py:1118
  149.2 0.0 copy-done.2
  149.2 0.0 copy-done.3
  149.2 0.0 copy-done.4
  149.2 1.7 %multiply_subtract_fusion = (f32[2,64,256]{2,1,0:T(8,128)}, f32[2,64,256]{2,1,0:T(8,128)}, f32[2,64,256]{2,1,0:T(8,128)}) fusion(f32[2,64,256]{2,1,0:T(8,128)S(1)} %copy-done.2, f32[2,64,256]{2,1,0:T(8,128)} %get-tuple-element.43, f32[2,64,256]{2,1,0:T(8,128)S(1)} %copy-done.3, f32[2,64,256]{2,1,0:T(8,128)S(1)} %copy-done.4), kind=kLoop, calls=%fused_computation.2 | loop fusion | flops 491520 | bytes 917504 | tf_op jit(solution)/shard_map/sub | solution.py:1197
  150.9 0.0 copy-start
  150.9 4.2 %convert_element_type.6 = f32[4,256,1024]{2,1,0:T(8,128)} convert(bf16[4,256,1024]{2,1,0:T(8,128)(2,1)} %get-tuple-element.29) | non-fusion elementwise | flops 1048576 | bytes 6291456 | tf_op jit(solution)/shard_map/convert_element_type | solution.py:1192
  155.2 0.0 copy-done
  155.2 0.0 copy-start.1
  155.2 2.5 %convert_element_type.7 = f32[4,256,1024]{2,1,0:T(8,128)} convert(bf16[4,256,1024]{2,1,0:T(8,128)(2,1)S(1)} %copy-done) | non-fusion elementwise | flops 1048576 | bytes 6291456 | tf_op jit(solution)/shard_map/convert_element_type | solution.py:1192
  157.6 0.0 copy-done.1
  157.6 0.7 copy.22
Async XLA Ops:
  100.4 48.8 %copy-start.2 = (f32[2,64,256]{2,1,0:T(8,128)S(1)}, f32[2,64,256]{2,1,0:T(8,128)}, u32[]{:S(2)}) copy-start(f32[2,64,256]{2,1,0:T(8,128)} %prefix.1) | copy-start | bytes 393220
  100.4 48.8 %copy-start.3 = (f32[2,64,256]{2,1,0:T(8,128)S(1)}, f32[2,64,256]{2,1,0:T(8,128)}, u32[]{:S(2)}) copy-start(f32[2,64,256]{2,1,0:T(8,128)} %param.18) | copy-start | bytes 393220
  100.4 48.8 %copy-start.4 = (f32[2,64,256]{2,1,0:T(8,128)S(1)}, f32[2,64,256]{2,1,0:T(8,128)}, u32[]{:S(2)}) copy-start(f32[2,64,256]{2,1,0:T(8,128)} %param.19) | copy-start | bytes 393220
  150.9 4.2 %copy-start = (bf16[4,256,1024]{2,1,0:T(8,128)(2,1)S(1)}, bf16[4,256,1024]{2,1,0:T(8,128)(2,1)}, u32[]{:S(2)}) copy-start(bf16[4,256,1024]{2,1,0:T(8,128)(2,1)} %get-tuple-element.30) | copy-start | bytes 6291460
  155.2 2.5 %copy-start.1 = (f32[2,64,256]{2,1,0:T(8,128)S(1)}, f32[2,64,256]{2,1,0:T(8,128)}, u32[]{:S(2)}) copy-start(f32[2,64,256]{2,1,0:T(8,128)} %get-tuple-element.43) | copy-start | bytes 393220
